TPU v7x, 512 devices: a whole 4x4x16 slice. The times are simulated.
512 devices in a mesh: row: 32 (over y, x, core), col: 16 (over z).
Axes of the slice: x: 4, y: 4, z: 16, core: 2. Of those that a mesh axis runs over, the one named last changes fastest.
Arguments:
- activations: bfloat16 [512, 12288], P('col', 'row'), may hold values from -6 to 6
- up_weight: bfloat16 [12288, 24576], P('row', 'col'), may hold values from -0.0546875 to 0.0546875
- down_weight: bfloat16 [24576, 12288], P('col', 'row'), may hold values from -0.0390625 to 0.0390625
- cotangent: bfloat16 [512, 12288], P('col', 'row'), may hold values from -6 to 6
Outputs:
- output: bfloat16 [512, 12288], P('col', 'row')
- grad_input: bfloat16 [512, 12288], P('col', 'row')
- grad_up: bfloat16 [12288, 24576], P('row', 'col')
- grad_down: bfloat16 [24576, 12288], P('col', 'row')
All inputs are finite; a program needn't handle non-finite values.
Results may differ from a plain program's by a relative error of at most 0.034.
Values may be sent and summed in bfloat16 or wider, within the bound.
No kernel may reach another device: no remote copies, remote signals or barrier semaphores. Data moves between devices by JAX's collectives and lax.ppermute only.
A program may use at most 64 MiB of HBM per device.

v0:
```python
import math

import jax
import jax.numpy as jnp
from jax import lax
from jax.sharding import PartitionSpec as P


def gelu_tanh(z):
    c = math.sqrt(2.0 / math.pi)
    return 0.5 * z * (1.0 + jnp.tanh(c * (z + 0.044715 * z * z * z)))


def gelu_slope(z):
    c = math.sqrt(2.0 / math.pi)
    t = jnp.tanh(c * (z + 0.044715 * z * z * z))
    return 0.5 * (1.0 + t) + 0.5 * z * (1.0 - t * t) * c * (1.0 + 3.0 * 0.044715 * z * z)


def per_device(activations, up_weight, down_weight, cotangent):
    act_panel = lax.all_gather(activations, "col", axis=0, tiled=True)
    cot_panel = lax.all_gather(cotangent, "col", axis=0, tiled=True)
    block = act_panel
    pre_act = lax.psum_scatter(
        jnp.dot(block, up_weight, preferred_element_type=jnp.float32).astype(jnp.bfloat16),
        "row",
        scatter_dimension=0,
        tiled=True,
    ).astype(jnp.float32)
    hidden = gelu_tanh(pre_act).astype(jnp.bfloat16)
    hidden_panel = lax.all_gather(hidden, "row", axis=0, tiled=True)
    block = hidden_panel
    output = lax.psum_scatter(
        jnp.dot(block, down_weight, preferred_element_type=jnp.float32).astype(jnp.bfloat16),
        "col",
        scatter_dimension=0,
        tiled=True,
    )
    block = cot_panel
    grad_hidden = lax.psum_scatter(
        jnp.einsum("td,fd->tf", block, down_weight, preferred_element_type=jnp.float32).astype(
            jnp.bfloat16
        ),
        "row",
        scatter_dimension=0,
        tiled=True,
    ).astype(jnp.float32)
    slope = (grad_hidden * gelu_slope(pre_act)).astype(jnp.bfloat16)
    slope_panel = lax.all_gather(slope, "row", axis=0, tiled=True)
    block = slope_panel
    grad_input = lax.psum_scatter(
        jnp.einsum("tf,df->td", block, up_weight, preferred_element_type=jnp.float32).astype(
            jnp.bfloat16
        ),
        "col",
        scatter_dimension=0,
        tiled=True,
    )
    grad_down = jnp.einsum(
        "tf,td->fd", hidden_panel, cot_panel, preferred_element_type=jnp.float32
    ).astype(jnp.bfloat16)
    grad_up = jnp.einsum(
        "td,tf->df", act_panel, slope_panel, preferred_element_type=jnp.float32
    ).astype(jnp.bfloat16)
    return (output, grad_input, grad_up, grad_down)


def solution(mesh):
    in_specs = (P("col", "row"), P("row", "col"), P("col", "row"), P("col", "row"))
    out_specs = (P("col", "row"), P("col", "row"), P("row", "col"), P("col", "row"))
    return jax.shard_map(
        per_device, mesh=mesh, in_specs=in_specs, out_specs=out_specs, check_vma=False
    )
```

profile of v0, /device:TPU:2, one launch (start us, length us, event | category | flops | bytes accessed | tf_op | source)
XLA Modules:
  0.0 523.3 jit_solution(8700262102075164963)
XLA Ops:
  7.2 0.0 copy-start
  7.2 0.0 reduce-scatter.5.cloned.1.call-start
  7.2 38.0 %all_gather.12 = bf16[512,384]{1,0:T(8,128)(2,1)S(1)} all-gather(bf16[32,384]{1,0:T(8,128)(2,1)} %param.4), channel_id=1, replica_groups=mesh['row'=32,'col'=16] {'col'}, dimensions={0}, use_global_device_ids=true | all-gather | bytes 417792 | tf_op jit(solution)/shard_map/all_gather | solution.py:21
  45.3 3.4 convolution_convert_fusion.1
  48.7 0.0 copy-start.2
  48.7 0.0 reduce-scatter.5.cloned.1.call-update
  48.7 0.0 reduce-scatter.9.cloned.1.call-start
  48.7 0.7 copy-done.2
  49.4 28.1 %all_gather.14 = bf16[512,384]{1,0:T(8,128)(2,1)S(1)} all-gather(bf16[32,384]{1,0:T(8,128)(2,1)S(1)} %copy-done.2), channel_id=1, replica_groups=mesh['row'=32,'col'=16] {'col'}, dimensions={0}, use_global_device_ids=true | all-gather | bytes 417792 | tf_op jit(solution)/shard_map/all_gather | solution.py:22
  77.5 0.0 copy-done
  77.5 2.2 convolution_convert_fusion
  79.7 0.0 reduce-scatter.9.cloned.1.call-update
  79.7 0.0 all-gather.3.cloned.1.call-start
  79.8 66.0 %reduce-scatter.5.cloned.1.call-done = bf16[16,1536]{1,0:T(8,128)(2,1)} async-done(((bf16[512,1536]{1,0:T(8,128)(2,1)}), bf16[16,1536]{1,0:T(8,128)(2,1)}) %reduce-scatter.5.cloned.1.call-update) | async-done | bytes 49168 | tf_op jit(solution)/shard_map/reduce_scatter | solution.py:24
  145.8 105.1 %reduce-scatter.9.cloned.1.call-done = bf16[16,1536]{1,0:T(8,128)(2,1)} async-done(((bf16[512,1536]{1,0:T(8,128)(2,1)}), bf16[16,1536]{1,0:T(8,128)(2,1)}) %reduce-scatter.9.cloned.1.call-update) | async-done | bytes 49168 | tf_op jit(solution)/shard_map/reduce_scatter | solution.py:40
  250.9 1.5 fusion.8
  252.4 0.0 all-gather.3.cloned.1.call-update
  252.5 0.0 all-gather.5.cloned.1.call-start
  252.5 0.5 all-gather.5.cloned.1.call-update
  253.0 0.0 copy-start.1
  253.1 0.0 reduce-scatter.7.cloned.1.call-start
  253.1 59.5 %all-gather.3.cloned.1.call-done = bf16[512,1536]{1,0:T(8,128)(2,1)} async-done(((bf16[16,1536]{1,0:T(8,128)(2,1)}), bf16[512,1536]{1,0:T(8,128)(2,1)}) %all-gather.3.cloned.1.call-update) | async-done | bytes 1572880 | tf_op jit(solution)/shard_map/all_gather | solution.py:31
  312.6 3.1 convolution_convert_fusion.5
  315.8 0.0 reduce-scatter.7.cloned.1.call-update
  315.8 0.0 reduce-scatter.11.cloned.1.call-start
  315.8 58.4 %all-gather.5.cloned.1.call-done = bf16[512,1536]{1,0:T(8,128)(2,1)} async-done(((bf16[16,1536]{1,0:T(8,128)(2,1)}), bf16[512,1536]{1,0:T(8,128)(2,1)}) %all-gather.5.cloned.1.call-update) | async-done | bytes 1572880 | tf_op jit(solution)/shard_map/all_gather | solution.py:49
  374.2 0.0 copy-done.1
  374.2 3.2 convolution_convert_fusion.4
  377.4 0.0 reduce-scatter.11.cloned.1.call-update
  377.4 2.4 fusion
  379.8 1.5 copy.8
  381.3 3.4 convolution_convert_fusion.2
  384.7 61.4 %reduce-scatter.7.cloned.1.call-done = bf16[32,384]{1,0:T(8,128)(2,1)} async-done(((bf16[512,384]{1,0:T(8,128)(2,1)}), bf16[32,384]{1,0:T(8,128)(2,1)}) %reduce-scatter.7.cloned.1.call-update) | async-done | bytes 24592 | tf_op jit(solution)/shard_map/reduce_scatter | solution.py:33
  446.2 70.3 %reduce-scatter.11.cloned.1.call-done = bf16[32,384]{1,0:T(8,128)(2,1)} async-done(((bf16[512,384]{1,0:T(8,128)(2,1)}), bf16[32,384]{1,0:T(8,128)(2,1)}) %reduce-scatter.11.cloned.1.call-update) | async-done | bytes 24592 | tf_op jit(solution)/shard_map/reduce_scatter | solution.py:51
Async XLA Ops:
  7.2 70.4 %copy-start = (bf16[1536,384]{1,0:T(8,128)(2,1)S(1)}, bf16[1536,384]{1,0:T(8,128)(2,1)}, u32[]{:S(2)}) copy-start(bf16[1536,384]{1,0:T(8,128)(2,1)} %param.6) | copy-start | bytes 3538948
  7.2 138.6 %reduce-scatter.5.cloned.1.call-start = ((), (), s32[]{:S(2)}) async-start(), calls=%async_computation.4 | async-start | bytes 1622016 | tf_op jit(solution)/shard_map/reduce_scatter | solution.py:24
  48.7 0.7 copy-start.2
  48.7 202.2 %reduce-scatter.9.cloned.1.call-start = ((), (), s32[]{:S(2)}) async-start(), calls=%async_computation.7 | async-start | bytes 1622016 | tf_op jit(solution)/shard_map/reduce_scatter | solution.py:40
  79.7 232.9 %all-gather.3.cloned.1.call-start = ((), (), s32[]{:S(2)}) async-start(), calls=%async_computation.5 | async-start | bytes 1622016 | tf_op jit(solution)/shard_map/all_gather | solution.py:31
  252.5 121.7 %all-gather.5.cloned.1.call-start = ((), (), s32[]{:S(2)}) async-start(), calls=%async_computation.8 | async-start | bytes 1622016 | tf_op jit(solution)/shard_map/all_gather | solution.py:49
  253.0 121.2 %copy-start.1 = (bf16[384,1536]{1,0:T(8,128)(2,1)S(1)}, bf16[384,1536]{1,0:T(8,128)(2,1)}, u32[]{:S(2)}) copy-start(bf16[384,1536]{1,0:T(8,128)(2,1)} %param.5) | copy-start | bytes 3538948
  253.1 193.1 %reduce-scatter.7.cloned.1.call-start = ((), (), s32[]{:S(2)}) async-start(), calls=%async_computation.6 | async-start | bytes 417792 | tf_op jit(solution)/shard_map/reduce_scatter | solution.py:33
  315.8 200.7 %reduce-scatter.11.cloned.1.call-start = ((), (), s32[]{:S(2)}) async-start(), calls=%async_computation.9 | async-start | bytes 417792 | tf_op jit(solution)/shard_map/reduce_scatter | solution.py:51
Sparse Core Ops, SparseCore 0:
  48.8 96.9 reduce-scatter.4
  150.2 100.6 reduce-scatter.8
  254.6 57.9 all-gather.2
  316.2 57.9 all-gather.4
  377.4 68.7 reduce-scatter.6
  449.6 66.8 reduce-scatter.10
where the time goes:
time: 524 us; the launch traced here: 523 us
  waiting for transfers between devices  421 us (80%)
  blocking collectives  66.1 us (13%)
  matrix products  17.7 us (3%)
  between operations  14.1 us (3%)
    reduce_scatter x1, waiting for transfers between devices, per_device(): lax.psum_scatter(jnp.einsum('td,fd->tf', block, down_weight, preferred_el...  105 us
    reduce_scatter x1, waiting for transfers between devices, per_device(): lax.psum_scatter(jnp.einsum('tf,df->td', block, up_weight, preferred_elem...  70.3 us
    reduce_scatter x1, waiting for transfers between devices, per_device(): lax.psum_scatter(jnp.dot(block, up_weight, preferred_element_type=jnp.flo...  66 us
    reduce_scatter x1, waiting for transfers between devices, per_device(): lax.psum_scatter(jnp.dot(block, down_weight, preferred_element_type=jnp.f...  61.4 us
    all_gather x1, waiting for transfers between devices, per_device(): hidden_panel = lax.all_gather(hidden, 'row', axis=0, tiled=True)  59.5 us
    all_gather x1, waiting for transfers between devices, per_device(): slope_panel = lax.all_gather(slope, 'row', axis=0, tiled=True)  58.4 us
    all_gather x1, blocking collectives, per_device(): act_panel = lax.all_gather(activations, 'col', axis=0, tiled=True)  38 us
    all_gather x1, blocking collectives, per_device(): cot_panel = lax.all_gather(cotangent, 'col', axis=0, tiled=True)  28.1 us
  transfers between devices with their start and end apart: 6, of which 6 were waited for; matrix products, arithmetic and copies ran while one was open for 3% of the time, Pallas kernels for 0%

commit v1 on v0

v1 whole, which is shorter than its diff:
```python
import math

import jax
import jax.numpy as jnp
from jax import lax
from jax.sharding import Mesh
from jax.sharding import PartitionSpec as P

BF16 = jnp.bfloat16
F32 = jnp.float32
COEF = math.sqrt(2.0 / math.pi)
PLANE = ("y", "x")
SWAP = [(0, 1), (1, 0)]


def gelu_and_slope(z):
    t = jnp.tanh(COEF * (z + 0.044715 * z * z * z))
    value = 0.5 * z * (1.0 + t)
    slope = 0.5 * (1.0 + t) + 0.5 * z * (1.0 - t * t) * COEF * (1.0 + 3.0 * 0.044715 * z * z)
    return value, slope


def dot(a, b):
    return jnp.dot(a, b, preferred_element_type=F32)


def dot_t(a, b):
    return jnp.einsum("tk,nk->tn", a, b, preferred_element_type=F32)


def dot_tok(a, b):
    return jnp.einsum("tm,tn->mn", a, b, preferred_element_type=F32)


def per_device(activations, up_weight, down_weight, cotangent):
    rows, width = activations.shape
    hid = up_weight.shape[1]
    core = lax.axis_index("core")
    zl = lax.axis_index("zl")

    both = jnp.concatenate([activations, cotangent], axis=1)
    panel = lax.all_gather(both, ("zh", "zl"), axis=0, tiled=True)
    tokens = panel.shape[0]
    half = tokens // 2

    def first(part):
        block = lax.dynamic_slice_in_dim(panel, part * half, half, 0)
        pre = dot(block[:, :width], up_weight).astype(BF16)
        grad = dot_t(block[:, width:], down_weight).astype(BF16)
        return jnp.concatenate([pre, grad], axis=1)

    away = first(1 - core)
    arrived = lax.ppermute(away, "core", SWAP)
    home = first(core)
    partial = (home.astype(F32) + arrived.astype(F32)).astype(BF16)

    got = lax.all_to_all(partial, PLANE, 0, 0, tiled=True)
    total = jnp.sum(got.reshape(16, half // 16, 2 * hid).astype(F32), axis=0)
    value, slope = gelu_and_slope(total[:, :hid])
    mine = jnp.concatenate(
        [value.astype(BF16), (total[:, hid:] * slope).astype(BF16)], axis=1
    )
    spread = jnp.broadcast_to(mine[None], (16,) + mine.shape).reshape(half, 2 * hid)
    own_half = lax.all_to_all(spread, PLANE, 0, 0, tiled=True)
    other_half = lax.ppermute(own_half, "core", SWAP)

    def second(block):
        out = dot(block[:, :hid], down_weight).astype(BF16)
        grad = dot_t(block[:, hid:], up_weight).astype(BF16)
        return jnp.concatenate([out, grad], axis=1)

    own_out = second(own_half)
    other_out = second(other_half)
    first_half = jnp.where(core == 0, own_out, other_out)
    second_half = jnp.where(core == 0, other_out, own_out)
    full = jnp.concatenate([first_half, second_half], axis=0)
    pairs = full.reshape(tokens // (2 * rows), 2, rows, 2 * width)
    send = lax.dynamic_index_in_dim(pairs, 1 - zl, 1, keepdims=False)
    keep = lax.dynamic_index_in_dim(pairs, zl, 1, keepdims=False)
    came = lax.ppermute(send, "zl", SWAP)

    hidden_all = jnp.concatenate(
        [jnp.where(core == 0, own_half, other_half), jnp.where(core == 0, other_half, own_half)],
        axis=0,
    )
    grad_down = dot_tok(hidden_all[:, :hid], panel[:, width:]).astype(BF16)
    grad_up = dot_tok(panel[:, :width], hidden_all[:, hid:]).astype(BF16)

    added = (keep.astype(F32) + came.astype(F32)).astype(BF16)
    parts = lax.all_to_all(added.reshape(half, 2 * width), "zh", 0, 0, tiled=True)
    result = jnp.sum(parts.reshape(8, rows, 2 * width).astype(F32), axis=0).astype(BF16)
    return (result[:, :width], result[:, width:], grad_up, grad_down)


def solution(mesh):
    fine = Mesh(mesh.devices.reshape(4, 4, 2, 8, 2), ("y", "x", "core", "zh", "zl"))
    row = ("y", "x", "core")
    col = ("zh", "zl")
    return jax.shard_map(
        per_device,
        mesh=fine,
        in_specs=(P(col, row), P(row, col), P(col, row), P(col, row)),
        out_specs=(P(col, row), P(col, row), P(row, col), P(col, row)),
        check_vma=False,
    )
```

time: 524 us -> 165 us (0.31)
  the two profiles are of different devices: /device:TPU:2 before, /device:TPU:64 now
where the time goes in v1:
time: 165 us; the launch traced here: 164 us
  blocking collectives  92.3 us (56%)
  waiting for transfers between devices  35.1 us (21%)
  starting transfers between devices  14.9 us (9%)
  matrix products  10.8 us (7%)
  other arithmetic  8.25 us (5%)
  local copies, waits for them, and re-layouts  2.27 us (1%)
    all_gather x1, blocking collectives, per_device(): panel = lax.all_gather(both, ('zh', 'zl'), axis=0, tiled=True)  37.1 us
    all_to_all x1, blocking collectives, per_device(): got = lax.all_to_all(partial, PLANE, 0, 0, tiled=True)  29.9 us
    all_to_all x1, blocking collectives, per_device(): own_half = lax.all_to_all(spread, PLANE, 0, 0, tiled=True)  25.3 us
    all_to_all x1, waiting for transfers between devices, per_device(): lax.all_to_all(added.reshape(half, 2 * width), 'zh', 0, 0, tiled=True)  19.5 us
    ppermute x1, waiting for transfers between devices, per_device(): came = lax.ppermute(send, 'zl', SWAP)  11.4 us
    all_to_all x1, starting transfers between devices, per_device(): lax.all_to_all(added.reshape(half, 2 * width), 'zh', 0, 0, tiled=True)  9.21 us
    dot_general x2, matrix products, dot_tok(): return jnp.einsum('tm,tn->mn', a, b, preferred_element_type=F32)  3.85 us
    dot_general x4, matrix products, dot_t(): return jnp.einsum('tk,nk->tn', a, b, preferred_element_type=F32)  3.51 us
  transfers between devices with their start and end apart: 4, of which 4 were waited for; matrix products, arithmetic and copies ran while one was open for 5% of the time, Pallas kernels for 0%

profile of v1, /device:TPU:64, one launch (start us, length us, event | category | flops | bytes accessed | tf_op | source)
XLA Modules:
  0.0 164.4 jit_solution(14635747113554831010)
XLA Ops:
  0.6 0.0 copy-start
  0.6 0.0 copy-start.1
  0.7 0.9 pad_maximum_fusion.7
  1.6 37.1 %all_gather.3 = bf16[512,768]{1,0:T(8,128)(2,1)S(1)} all-gather(bf16[32,768]{1,0:T(8,128)(2,1)S(1)} %pad_maximum_fusion.7), channel_id=1, replica_groups=mesh['y'=4,'x'=4,'core'=2,'zh'=8,'zl'=2] {'zh','zl'}, dimensions={0}, use_global_device_ids=true | all-gather | bytes 835584 | tf_op jit(solution)/shard_map/all_gather | solution.py:42
  38.7 0.0 copy-start.3
  38.7 0.0 copy-done
  38.7 0.6 convolution_convert_fusion.3
  39.3 0.0 copy-done.1
  39.3 0.6 convolution_convert_fusion.2
  39.9 1.4 pad_maximum_fusion.2
  41.2 1.9 %collective-permute-start = (bf16[256,3072]{1,0:T(8,128)(2,1)}, bf16[256,3072]{1,0:T(8,128)(2,1)}, u32[]{:S(2)}, u32[]{:S(2)}) collective-permute-start(bf16[256,3072]{1,0:T(8,128)(2,1)} %pad_maximum_fusion.2), channel_id=1, source_target_pairs={{0,16},{16,0},{1,17},{17,1},{2,18},{18,2},{3,19},{19,3},{4,20},{20... | collective-permute-start | bytes 4718600 | tf_op jit(solution)/shard_map/ppermute | solution.py:53
  43.2 0.6 convolution_convert_fusion.4
  43.8 0.0 copy-done.3
  43.8 0.6 convolution_convert_fusion.5
  44.4 2.5 %collective-permute-done = bf16[256,3072]{1,0:T(8,128)(2,1)} collective-permute-done((bf16[256,3072]{1,0:T(8,128)(2,1)}, bf16[256,3072]{1,0:T(8,128)(2,1)}, u32[]{:S(2)}, u32[]{:S(2)}) %collective-permute-start) | collective-permute-done | bytes 1572896 | tf_op jit(solution)/shard_map/ppermute | solution.py:53
  46.9 1.9 %add_convert_fusion = bf16[256,3072]{1,0:T(8,128)(2,1)S(1)} fusion(bf16[256,3072]{1,0:T(8,128)(2,1)} %collective-permute-done, bf16[256,1536]{1,0:T(8,128)(2,1)S(1)} %convolution_convert_fusion.4, bf16[256,1536]{1,0:T(8,128)(2,1)S(1)} %convolution_convert_fusion.5), kind=kLoop, calls=%fused_computation.3 | loop fusion | flops 5505024 | bytes 4718592 | tf_op jit(solution)/shard_map/convert_element_type | solution.py:55
  48.8 29.9 %all_to_all.24 = bf16[16,16,3072]{2,1,0:T(8,128)(2,1)S(1)} all-to-all(bf16[16,16,3072]{2,1,0:T(8,128)(2,1)S(1)} %bitcast.21), channel_id=1, replica_groups=mesh['y'=4,'x'=4,'core'=2,'zh'=8,'zl'=2] {'y','x'}, dimensions={0} | all-to-all | bytes 3145728 | tf_op jit(solution)/shard_map/all_to_all | solution.py:57
  78.7 0.2 convert_reduce_fusion
  78.9 0.1 multiply_convert_fusion
  79.0 0.2 broadcast_in_dim.2
  79.2 25.3 %all_to_all.25 = bf16[16,16,3072]{2,1,0:T(8,128)(2,1)S(1)} all-to-all(bf16[16,16,3072]{2,1,0:T(8,128)(2,1)S(1)} %broadcast_in_dim.2), channel_id=1, replica_groups=mesh['y'=4,'x'=4,'core'=2,'zh'=8,'zl'=2] {'y','x'}, dimensions={0} | all-to-all | bytes 3145728 | tf_op jit(solution)/shard_map/all_to_all | solution.py:64
  104.4 1.9 %collective-permute-start.1 = (bf16[256,3072]{1,0:T(8,128)(2,1)S(1)}, bf16[256,3072]{1,0:T(8,128)(2,1)}, u32[]{:S(2)}, u32[]{:S(2)}) collective-permute-start(bf16[256,3072]{1,0:T(8,128)(2,1)S(1)} %bitcast.18), channel_id=1, source_target_pairs={{0,16},{16,0},{1,17},{17,1},{2,18},{18,2},{3,19},{19,3},{4,20},{20... | collective-permute-start | bytes 4718600 | tf_op jit(solution)/shard_map/ppermute | solution.py:65
  106.4 0.0 copy-start.2
  106.4 0.6 convolution_convert_fusion.8
  107.0 0.7 copy-done.2
  107.6 0.6 convolution_convert_fusion.9
  108.2 1.6 %collective-permute-done.1 = bf16[256,3072]{1,0:T(8,128)(2,1)} collective-permute-done((bf16[256,3072]{1,0:T(8,128)(2,1)S(1)}, bf16[256,3072]{1,0:T(8,128)(2,1)}, u32[]{:S(2)}, u32[]{:S(2)}) %collective-permute-start.1) | collective-permute-done | bytes 1572896 | tf_op jit(solution)/shard_map/ppermute | solution.py:65
  109.9 1.7 %convolution_convert_fusion.6 = bf16[256,384]{1,0:T(8,128)(2,1)S(1)} fusion(bf16[384,1536]{1,0:T(8,128)(2,1)S(1)} %copy-done, bf16[256,3072]{1,0:T(8,128)(2,1)} %collective-permute-done.1), kind=kOutput, calls=%fused_computation.16 | convolution fusion | flops 302088192 | bytes 2162688 | tf_op jit(solution)/shard_map/tk,nk->tn/dot_general | solution.py:28
  111.6 1.7 %convolution_convert_fusion.7 = bf16[256,384]{1,0:T(8,128)(2,1)S(1)} fusion(bf16[1536,384]{1,0:T(8,128)(2,1)S(1)} %copy-done.2, bf16[256,3072]{1,0:T(8,128)(2,1)} %collective-permute-done.1), kind=kOutput, calls=%fused_computation.17 | convolution fusion | flops 302088192 | bytes 2162688 | tf_op jit(solution)/shard_map/dot_general | solution.py:24
  113.3 0.1 broadcast_select_fusion.3
  113.4 0.1 pad_maximum_fusion.3
  113.5 0.8 dynamic-slice_bitcast_fusion
  114.3 1.9 %collective-permute-start.2 = (bf16[8,32,768]{2,1,0:T(8,128)(2,1)}, bf16[8,32,768]{2,1,0:T(8,128)(2,1)}, u32[]{:S(2)}, u32[]{:S(2)}) collective-permute-start(bf16[8,32,768]{2,1,0:T(8,128)(2,1)} %dynamic-slice_bitcast_fusion), channel_id=1, source_target_pairs={{0,1},{1,0},{2,3},{3,2},{4,5},{5,4},{6,7},{7,6},{8,9},{9,8},{10,11... | collective-permute-start | bytes 1179656 | tf_op jit(solution)/shard_map/ppermute | solution.py:80
  116.2 11.4 %collective-permute-done.2 = bf16[8,32,768]{2,1,0:T(8,128)(2,1)} collective-permute-done((bf16[8,32,768]{2,1,0:T(8,128)(2,1)}, bf16[8,32,768]{2,1,0:T(8,128)(2,1)}, u32[]{:S(2)}, u32[]{:S(2)}) %collective-permute-start.2) | collective-permute-done | bytes 393248 | tf_op jit(solution)/shard_map/ppermute | solution.py:80
  127.6 1.8 %fusion.7 = bf16[8,32,768]{2,1,0:T(8,128)(2,1)} fusion(bf16[8,32,768]{2,1,0:T(8,128)(2,1)} %collective-permute-done.2, bf16[8,2,32,768]{3,2,1,0:T(8,128)(2,1)S(1)} %bitcast.23, s32[]{:T(128)S(6)} %select_n.42), kind=kLoop, calls=%fused_computation.26 | loop fusion | flops 786432 | bytes 1179652 | tf_op jit(solution)/shard_map/convert_element_type | solution.py:89
  129.5 9.2 %all-to-all-start.2 = ((bf16[8,32,768]{2,1,0:T(8,128)(2,1)}), bf16[8,32,768]{2,1,0:T(8,128)(2,1)S(1)}, u32[]{:S(2)}, u32[]{:S(2)}) async-start(bf16[8,32,768]{2,1,0:T(8,128)(2,1)} %fusion.7), calls=%async_computation.2 | async-start | bytes 786432 | tf_op jit(solution)/shard_map/all_to_all | solution.py:90
  138.7 0.0 copy-start.4
  138.7 1.7 %broadcast_select_fusion = (bf16[256,3072]{1,0:T(8,128)(2,1)S(1)}, bf16[256,3072]{1,0:T(8,128)(2,1)S(1)}) fusion(bf16[256,3072]{1,0:T(8,128)(2,1)} %collective-permute-done.1, pred[]{:T(512)S(6)} %eq.2, bf16[16,16,3072]{2,1,0:T(8,128)(2,1)S(1)} %all_to_all.25), kind=kLoop, calls=%fused_computation.14 | loop fusion | flops 1572864 | bytes 6291457 | tf_op jit(solution)/shard_map/jit(_where)/select_n | solution.py:83
  140.4 0.0 copy-done.4
  140.4 2.0 %convolution_convert_fusion = bf16[1536,384]{1,0:T(8,128)(2,1)} fusion(bf16[256,3072]{1,0:T(8,128)(2,1)S(1)} %get-tuple-element.4, bf16[256,3072]{1,0:T(8,128)(2,1)S(1)} %get-tuple-element.5, bf16[512,768]{1,0:T(8,128)(2,1)S(1)} %copy-done.4), kind=kOutput, calls=%fused_computation.4 | convolution fusion | flops 607715328 | bytes 4718592 | tf_op jit(solution)/shard_map/tm,tn->mn/dot_general | solution.py:32
  142.4 1.8 %convolution_convert_fusion.1 = bf16[384,1536]{1,0:T(8,128)(2,1)} fusion(bf16[256,3072]{1,0:T(8,128)(2,1)S(1)} %get-tuple-element.5, bf16[256,3072]{1,0:T(8,128)(2,1)S(1)} %get-tuple-element.4, bf16[512,768]{1,0:T(8,128)(2,1)S(1)} %copy-done.4), kind=kOutput, calls=%fused_computation.5 | convolution fusion | flops 607715328 | bytes 4718592 | tf_op jit(solution)/shard_map/tm,tn->mn/dot_general | solution.py:32
  144.3 19.5 %all-to-all-done.2 = bf16[8,32,768]{2,1,0:T(8,128)(2,1)S(1)} async-done(((bf16[8,32,768]{2,1,0:T(8,128)(2,1)}), bf16[8,32,768]{2,1,0:T(8,128)(2,1)S(1)}, u32[]{:S(2)}, u32[]{:S(2)}) %all-to-all-start.2) | async-done | bytes 393248 | tf_op jit(solution)/shard_map/all_to_all | solution.py:90
  163.7 0.1 reduce_sum.22
  163.8 0.6 fusion.25
  (1 shorter events, 0.0 us)
Async XLA Ops:
  0.6 38.0 %copy-start = (bf16[384,1536]{1,0:T(8,128)(2,1)S(1)}, bf16[384,1536]{1,0:T(8,128)(2,1)}, u32[]{:S(2)}) copy-start(bf16[384,1536]{1,0:T(8,128)(2,1)} %param.5) | copy-start | bytes 3538948
  0.6 38.6 %copy-start.1 = (bf16[1536,384]{1,0:T(8,128)(2,1)S(1)}, bf16[1536,384]{1,0:T(8,128)(2,1)}, u32[]{:S(2)}) copy-start(bf16[1536,384]{1,0:T(8,128)(2,1)} %param.6) | copy-start | bytes 3538948
  38.7 5.1 %copy-start.3 = (bf16[512,768]{1,0:T(8,128)(2,1)}, bf16[512,768]{1,0:T(8,128)(2,1)S(1)}, u32[]{:S(2)}) copy-start(bf16[512,768]{1,0:T(8,128)(2,1)S(1)} %all_gather.3) | copy-start | bytes 2359300
  41.2 5.6 %collective-permute-start = (bf16[256,3072]{1,0:T(8,128)(2,1)}, bf16[256,3072]{1,0:T(8,128)(2,1)}, u32[]{:S(2)}, u32[]{:S(2)}) collective-permute-start(bf16[256,3072]{1,0:T(8,128)(2,1)} %pad_maximum_fusion.2), channel_id=1, source_target_pairs={{0,16},{16,0},{1,17},{17,1},{2,18},{18,2},{3,19},{19,3},{4,20},{20... | collective-permute-start | bytes 4718600 | tf_op jit(solution)/shard_map/ppermute | solution.py:53
  104.4 5.4 %collective-permute-start.1 = (bf16[256,3072]{1,0:T(8,128)(2,1)S(1)}, bf16[256,3072]{1,0:T(8,128)(2,1)}, u32[]{:S(2)}, u32[]{:S(2)}) collective-permute-start(bf16[256,3072]{1,0:T(8,128)(2,1)S(1)} %bitcast.18), channel_id=1, source_target_pairs={{0,16},{16,0},{1,17},{17,1},{2,18},{18,2},{3,19},{19,3},{4,20},{20... | collective-permute-start | bytes 4718600 | tf_op jit(solution)/shard_map/ppermute | solution.py:65
  106.4 1.3 copy-start.2
  114.3 13.4 %collective-permute-start.2 = (bf16[8,32,768]{2,1,0:T(8,128)(2,1)}, bf16[8,32,768]{2,1,0:T(8,128)(2,1)}, u32[]{:S(2)}, u32[]{:S(2)}) collective-permute-start(bf16[8,32,768]{2,1,0:T(8,128)(2,1)} %dynamic-slice_bitcast_fusion), channel_id=1, source_target_pairs={{0,1},{1,0},{2,3},{3,2},{4,5},{5,4},{6,7},{7,6},{8,9},{9,8},{10,11... | collective-permute-start | bytes 1179656 | tf_op jit(solution)/shard_map/ppermute | solution.py:80
  129.5 34.2 %all-to-all-start.2 = ((bf16[8,32,768]{2,1,0:T(8,128)(2,1)}), bf16[8,32,768]{2,1,0:T(8,128)(2,1)S(1)}, u32[]{:S(2)}, u32[]{:S(2)}) async-start(bf16[8,32,768]{2,1,0:T(8,128)(2,1)} %fusion.7), calls=%async_computation.2 | async-start | bytes 786432 | tf_op jit(solution)/shard_map/all_to_all | solution.py:90
  138.7 1.7 %copy-start.4 = (bf16[512,768]{1,0:T(8,128)(2,1)S(1)}, bf16[512,768]{1,0:T(8,128)(2,1)}, u32[]{:S(2)}) copy-start(bf16[512,768]{1,0:T(8,128)(2,1)} %copy-done.3) | copy-start | bytes 2359300

commit v2 on v1

v2 whole, which is shorter than its diff:
```python
import math

import jax
import jax.numpy as jnp
from jax import lax
from jax.experimental import pallas as pl
from jax.experimental.pallas import tpu as pltpu
from jax.sharding import Mesh
from jax.sharding import PartitionSpec as P

BF16 = jnp.bfloat16
F32 = jnp.float32
COEF = math.sqrt(2.0 / math.pi)
PLANE = ("y", "x")
COL = ("zh", "zl")
SWAP = [(0, 1), (1, 0)]
EVEN = [(z, z ^ 1) for z in range(16)]
ODD = [(z, (((z - 1) ^ 1) + 1) % 16) for z in range(16)]
TILE = 256
PIECES = 4
MIB = 1024 * 1024
VMEM = pl.BlockSpec(memory_space=pltpu.VMEM)
SMEM = pl.BlockSpec(memory_space=pltpu.SMEM)


def gelu_and_slope(z):
    t = jnp.tanh(COEF * (z + 0.044715 * z * z * z))
    value = 0.5 * z * (1.0 + t)
    slope = 0.5 * (1.0 + t) + 0.5 * z * (1.0 - t * t) * COEF * (1.0 + 3.0 * 0.044715 * z * z)
    return value, slope


def matmul(a, b, left, right):
    return lax.dot_general(a, b, (((left,), (right,)), ((), ())), preferred_element_type=F32)


def call(kernel, out_shape, flops, *args, scratch=()):
    specs = [SMEM if a.dtype == jnp.int32 else VMEM for a in args]
    size = sum(a.size * a.dtype.itemsize for a in args) + sum(
        math.prod(o.shape) * o.dtype.itemsize for o in out_shape
    )
    return pl.pallas_call(
        kernel,
        out_shape=out_shape,
        in_specs=specs,
        out_specs=[VMEM] * len(out_shape),
        scratch_shapes=scratch,
        compiler_params=pltpu.CompilerParams(vmem_limit_bytes=10 * MIB),
        cost_estimate=pl.CostEstimate(flops=flops, bytes_accessed=size, transcendentals=0),
    )(*args)


def shape(*dims):
    return jax.ShapeDtypeStruct(dims, BF16)


def pick_kernel(place_ref, pair, out):
    part = out.shape[0]
    rows, cols = 2 * part, pair.shape[1]
    core = place_ref[0]
    mine = pl.multiple_of(core * rows + core * part, part)
    theirs = pl.multiple_of((1 - core) * rows + core * part, part)
    out[:, :cols] = pair[pl.ds(mine, part), :]
    out[:, cols:] = pair[pl.ds(theirs, part), :]


def first_kernel(panel, up, down, up2, down2, out):
    width, hid = up.shape
    act, cot, act2, cot2 = [panel[:, q * width : (q + 1) * width] for q in range(4)]
    for t in range(0, hid, TILE):
        span = slice(t, t + TILE)
        out[:, span] = (
            matmul(act, up[:, span], 1, 0) + matmul(act2, up2[:, span], 1, 0)
        ).astype(BF16)
        out[:, hid + t : hid + t + TILE] = (
            matmul(cot, down[span, :], 1, 1) + matmul(cot2, down2[span, :], 1, 1)
        ).astype(BF16)


def part_rows(place_ref, full, send, keep):
    part = 16
    zl = place_ref[1]
    for q in range(full.shape[0] // (2 * part)):
        base = 2 * q * part
        place = slice(q * part, (q + 1) * part)
        send[place, :] = full[pl.ds(pl.multiple_of(base + (1 - zl) * part, part), part), :]
        keep[place, :] = full[pl.ds(pl.multiple_of(base + zl * part, part), part), :]


def output_kernel(place_ref, block, down, down2, send, keep, full):
    hid, width = down.shape
    full[:, :width] = matmul(block[:, :hid], down[...], 1, 0).astype(BF16)
    full[:, width:] = matmul(block[:, :hid], down2[...], 1, 0).astype(BF16)
    part_rows(place_ref, full, send, keep)


def input_kernel(place_ref, block, up, up2, send, keep, full):
    width, hid = up.shape
    full[:, :width] = matmul(block[:, hid:], up[...], 1, 1).astype(BF16)
    full[:, width:] = matmul(block[:, hid:], up2[...], 1, 1).astype(BF16)
    part_rows(place_ref, full, send, keep)


def pair_kernel(keep_a, came_a, keep_b, came_b, out):
    cols = keep_a.shape[1]
    out[:, :cols] = (keep_a[...].astype(F32) + came_a[...].astype(F32)).astype(BF16)
    out[:, cols:] = (keep_b[...].astype(F32) + came_b[...].astype(F32)).astype(BF16)


def stage_kernel(_, own, panel, *outs):
    *copies, theirs = outs
    cols = copies[0].shape[1]
    for q, copy in enumerate(copies):
        copy[...] = own[:, q * cols : (q + 1) * cols]
    theirs[...] = panel[:, theirs.shape[1] :]


def sum_kernel(parts, out):
    rows = out.shape[0]
    total = parts[:rows, :].astype(F32)
    for q in range(1, parts.shape[0] // rows):
        total = total + parts[q * rows : (q + 1) * rows, :].astype(F32)
    out[...] = total.astype(BF16)


def last_kernel(place_ref, both, output, grad_input):
    rows, width = output.shape
    part = rows // 2
    core = place_ref[0]
    for source in range(2):
        place = slice(source * part, (source + 1) * part)
        own = core == source
        output[place, :] = jnp.where(own, both[place, :width], both[place, width : 2 * width])
        grad_input[place, :] = jnp.where(
            own, both[place, 2 * width : 3 * width], both[place, 3 * width :]
        )


def grads_kernel(panel, panel2, own, *refs):
    *others, grad_up, grad_down = refs
    width, hid = grad_up.shape
    act, cot = panel[:, :width], panel[:, width : 2 * width]
    act2, cot2 = panel2[:, :width], panel2[:, width:]
    piece = others[0].shape[1]

    def other(begin):
        return others[begin // piece][:, begin % piece : begin % piece + TILE]

    for j in range(0, hid, TILE):
        grad_down[j : j + TILE, :] = (
            matmul(own[:, j : j + TILE], cot, 0, 0) + matmul(other(j), cot2, 0, 0)
        ).astype(BF16)
        grad_up[:, j : j + TILE] = (
            matmul(act, own[:, hid + j : hid + j + TILE], 0, 0)
            + matmul(act2, other(hid + j), 0, 0)
        ).astype(BF16)


def per_device(activations, up, down, cotangent):
    rows, width = activations.shape
    hid = up.shape[1]
    place = jnp.stack([lax.axis_index("core"), lax.axis_index("zl")]).astype(jnp.int32)
    part = rows // 2
    half = 16 * part
    members = 16
    work = 8 * half * width * hid

    up2 = lax.ppermute(up, "core", SWAP)
    down2 = lax.ppermute(down, "core", SWAP)
    pair = lax.all_gather(
        jnp.concatenate([activations, cotangent], axis=1), "core", axis=0, tiled=True
    )
    (mine,) = call(pick_kernel, [shape(part, 4 * width)], 0, place, pair)
    panel = lax.all_gather(mine, COL, axis=0, tiled=True)

    (partial,) = call(
        first_kernel, [shape(half, 2 * hid)], work, panel, up, down, up2, down2
    )

    got = lax.all_to_all(partial, PLANE, 0, 0, tiled=True)
    total = jnp.sum(got.reshape(members, half // members, 2 * hid).astype(F32), axis=0)
    value, slope = gelu_and_slope(total[:, :hid])
    sixteen = jnp.concatenate(
        [value.astype(BF16), (total[:, hid:] * slope).astype(BF16)], axis=1
    )
    spread = jnp.broadcast_to(sixteen[None], (members,) + sixteen.shape).reshape(half, 2 * hid)
    own = lax.all_to_all(spread, PLANE, 0, 0, tiled=True)

    def second(kernel, *args):
        outs = [shape(half // 2, 2 * width)] * 2
        return call(kernel, outs, work // 2, *args, scratch=[pltpu.VMEM((half, 2 * width), BF16)])

    send_out, keep_out = second(output_kernel, place, own, down, down2)
    came_out = lax.ppermute(send_out, COL, EVEN)
    send_in, keep_in = second(input_kernel, place, own, up, up2)
    came_in = lax.ppermute(send_in, COL, ODD)
    (added,) = call(
        pair_kernel, [shape(half // 2, 4 * width)], 0, keep_out, came_out, keep_in, came_in
    )
    gathered = lax.all_to_all(added, "zh", 0, 0, tiled=True)

    pieces = call(
        stage_kernel, [shape(half, 2 * width)] * (PIECES + 1), work // 4, added, own, panel
    )
    *others, panel2 = [lax.ppermute(piece, "core", SWAP) for piece in pieces]
    grad_up, grad_down = call(
        grads_kernel,
        [shape(width, hid), shape(hid, width)],
        work,
        panel,
        panel2,
        own,
        *others,
    )

    gathered, grad_up, grad_down = lax.optimization_barrier((gathered, grad_up, grad_down))
    (summed,) = call(sum_kernel, [shape(part, 4 * width)], 0, gathered)
    both = lax.all_gather(summed, "core", axis=0, tiled=True)
    output, grad_input = call(last_kernel, [shape(rows, width)] * 2, 0, place, both)
    return (output, grad_input, grad_up, grad_down)


def solution(mesh):
    fine = Mesh(mesh.devices.reshape(4, 4, 2, 8, 2), ("y", "x", "core", "zh", "zl"))
    row = ("y", "x", "core")
    return jax.shard_map(
        per_device,
        mesh=fine,
        in_specs=(P(COL, row), P(row, COL), P(COL, row), P(COL, row)),
        out_specs=(P(COL, row), P(COL, row), P(row, COL), P(COL, row)),
        check_vma=False,
    )
```

time: 165 us -> 142 us (0.86)
  the two profiles are of different devices: /device:TPU:64 before, /device:TPU:1 now
where the time goes in v2:
time: 142 us; the launch traced here: 141 us
  blocking collectives  73.6 us (52%)
  starting transfers between devices  44.3 us (31%)
  Pallas kernels  14.3 us (10%)
  waiting for transfers between devices  5.44 us (4%)
  local copies, waits for them, and re-layouts  1.45 us (1%)
    all_gather x1, blocking collectives, per_device(): panel = lax.all_gather(mine, COL, axis=0, tiled=True)  27.6 us
    all_to_all x1, blocking collectives, per_device(): got = lax.all_to_all(partial, PLANE, 0, 0, tiled=True)  22.4 us
    ppermute x5, starting transfers between devices, per_device(): *others, panel2 = [lax.ppermute(piece, 'core', SWAP) for piece in pieces]  20.7 us
    all_to_all x1, blocking collectives, per_device(): own = lax.all_to_all(spread, PLANE, 0, 0, tiled=True)  17.8 us
    pallas_call x9, Pallas kernels, call(): pl.pallas_call(kernel, out_shape=out_shape, in_specs=specs, out_specs=[VM...  14.3 us
    ppermute x1, starting transfers between devices, per_device(): up2 = lax.ppermute(up, 'core', SWAP)  8.92 us
    all_to_all x1, starting transfers between devices, per_device(): gathered = lax.all_to_all(added, 'zh', 0, 0, tiled=True)  8.02 us
    all_gather x1, blocking collectives, per_device(): both = lax.all_gather(summed, 'core', axis=0, tiled=True)  3.77 us
  transfers between devices with their start and end apart: 10, of which 3 were waited for; matrix products, arithmetic and copies ran while one was open for 1% of the time, Pallas kernels for 4%

profile of v2, /device:TPU:1, one launch (start us, length us, event | category | flops | bytes accessed | tf_op | source)
XLA Modules:
  0.0 141.1 jit_solution(10536296394063073050)
XLA Ops:
  0.6 0.0 copy-start
  0.6 8.9 %collective-permute-start = (bf16[384,1536]{1,0:T(8,128)(2,1)}, bf16[384,1536]{1,0:T(8,128)(2,1)}, u32[]{:S(2)}, u32[]{:S(2)}) collective-permute-start(bf16[384,1536]{1,0:T(8,128)(2,1)} %up.3), channel_id=1, source_target_pairs={{0,16},{16,0},{1,17},{17,1},{2,18},{18,2},{3,19},{19,3},{4,20},{20... | collective-permute-start | bytes 3538952 | tf_op jit(solution)/shard_map/ppermute | solution.py:168
  9.6 1.9 %collective-permute-start.1 = (bf16[1536,384]{1,0:T(8,128)(2,1)}, bf16[1536,384]{1,0:T(8,128)(2,1)S(1)}, u32[]{:S(2)}, u32[]{:S(2)}) collective-permute-start(bf16[1536,384]{1,0:T(8,128)(2,1)} %down.3), channel_id=1, source_target_pairs={{0,16},{16,0},{1,17},{17,1},{2,18},{18,2},{3,19},{19,3},{4,20},{20... | collective-permute-start | bytes 3538952 | tf_op jit(solution)/shard_map/ppermute | solution.py:169
  11.5 0.8 pad_maximum_fusion.1
  12.3 2.1 %all_gather.9.pair = bf16[64,768]{1,0:T(8,128)(2,1)S(1)} all-gather(bf16[32,768]{1,0:T(8,128)(2,1)S(1)} %pad_maximum_fusion.1), channel_id=1, replica_groups=mesh['y'=4,'x'=4,'core'=2,'zh'=8,'zl'=2] {'core'}, dimensions={0}, use_global_device_ids=true | all-gather | bytes 147456 | tf_op jit(solution)/shard_map/all_gather | solution.py:170
  14.4 0.1 pad_add_fusion.place_ref
  14.5 0.6 shard_map.75
  15.0 27.6 %all_gather.10.panel = bf16[256,1536]{1,0:T(8,128)(2,1)S(1)} all-gather(bf16[16,1536]{1,0:T(8,128)(2,1)S(1)} %shard_map.75), channel_id=1, replica_groups=mesh['y'=4,'x'=4,'core'=2,'zh'=8,'zl'=2] {'zh','zl'}, dimensions={0}, use_global_device_ids=true | all-gather | bytes 835584 | tf_op jit(solution)/shard_map/all_gather | solution.py:174
  42.6 0.0 collective-permute-done.up2
  42.6 0.0 collective-permute-done.1.down2
  42.6 0.0 copy-done
  42.6 0.0 copy-start.1
  42.6 1.3 copy-done.1
  43.9 0.0 copy-start.3
  43.9 3.5 %shard_map.76 = bf16[256,3072]{1,0:T(8,128)(2,1)S(1)} custom-call(bf16[256,1536]{1,0:T(8,128)(2,1)S(1)} %all_gather.10.panel, bf16[384,1536]{1,0:T(8,128)(2,1)S(1)} %copy-done, bf16[1536,384]{1,0:T(8,128)(2,1)S(1)} %copy-done.1, bf16[384,1536]{1,0:T(8,128)(2,1)} %collective-permute-done.up2, bf16[1536,384]{1,0:T(8,128)(2,1)S(1)} %collective-permute-done.1.down2), custom_call_target="tpu_custom_call" | custom-call | flops 1207959552 | bytes 7077888 | tf_op jit(solution)/shard_map/pallas_call | solution.py:42
  47.4 0.0 copy-done.3
  47.4 22.4 %all_to_all.29 = bf16[16,16,3072]{2,1,0:T(8,128)(2,1)S(1)} all-to-all(bf16[16,16,3072]{2,1,0:T(8,128)(2,1)S(1)} %bitcast.10), channel_id=1, replica_groups=mesh['y'=4,'x'=4,'core'=2,'zh'=8,'zl'=2] {'y','x'}, dimensions={0} | all-to-all | bytes 3145728 | tf_op jit(solution)/shard_map/all_to_all | solution.py:180
  69.8 0.2 convert_reduce_fusion
  70.0 0.1 multiply_convert_fusion
  70.1 0.2 broadcast_in_dim.2
  70.3 17.8 %all_to_all.30 = bf16[16,16,3072]{2,1,0:T(8,128)(2,1)S(1)} all-to-all(bf16[16,16,3072]{2,1,0:T(8,128)(2,1)S(1)} %broadcast_in_dim.2), channel_id=1, replica_groups=mesh['y'=4,'x'=4,'core'=2,'zh'=8,'zl'=2] {'y','x'}, dimensions={0} | all-to-all | bytes 3145728 | tf_op jit(solution)/shard_map/all_to_all | solution.py:187
  88.1 0.0 copy-start.2
  88.1 2.4 %shard_map.78 = (bf16[128,768]{1,0:T(8,128)(2,1)S(1)}, bf16[128,768]{1,0:T(8,128)(2,1)S(1)}) custom-call(s32[2]{0:T(128)S(1)} %pad_add_fusion.place_ref, bf16[256,3072]{1,0:T(8,128)(2,1)S(1)} %bitcast.6, bf16[384,1536]{1,0:T(8,128)(2,1)S(1)} %copy-done, bf16[384,1536]{1,0:T(8,128)(2,1)} %collective-permute-done.up2), custom_call_target="tpu_custom_call" | custom-call | flops 603979776 | bytes 4325384 | tf_op jit(solution)/shard_map/pallas_call | solution.py:42
  90.5 2.4 %collective-permute-start.3 = (bf16[128,768]{1,0:T(8,128)(2,1)S(1)}, bf16[128,768]{1,0:T(8,128)(2,1)S(1)}, u32[]{:S(2)}, u32[]{:S(2)}) collective-permute-start(bf16[128,768]{1,0:T(8,128)(2,1)S(1)} %get-tuple-element.23), channel_id=1, source_target_pairs={{0,15},{1,2},{2,1},{3,4},{4,3},{5,6},{6,5},{7,8},{8,7},{9,10},{10,... | collective-permute-start | bytes 589832 | tf_op jit(solution)/shard_map/ppermute | solution.py:196
  92.9 0.0 copy-done.2
  92.9 0.0 copy-done.4
  93.0 1.6 %shard_map.77 = (bf16[128,768]{1,0:T(8,128)(2,1)S(1)}, bf16[128,768]{1,0:T(8,128)(2,1)S(1)}) custom-call(s32[2]{0:T(128)S(1)} %pad_add_fusion.place_ref, bf16[256,3072]{1,0:T(8,128)(2,1)S(1)} %bitcast.7, bf16[1536,384]{1,0:T(8,128)(2,1)S(1)} %copy-done.2, bf16[1536,384]{1,0:T(8,128)(2,1)S(1)} %copy-done.4), custom_call_target="tpu_custom_call" | custom-call | flops 603979776 | bytes 4325384 | tf_op jit(solution)/shard_map/pallas_call | solution.py:42
  94.5 2.3 %collective-permute-start.2 = (bf16[128,768]{1,0:T(8,128)(2,1)S(1)}, bf16[128,768]{1,0:T(8,128)(2,1)S(1)}, u32[]{:S(2)}, u32[]{:S(2)}) collective-permute-start(bf16[128,768]{1,0:T(8,128)(2,1)S(1)} %get-tuple-element.21), channel_id=1, source_target_pairs={{0,1},{1,0},{2,3},{3,2},{4,5},{5,4},{6,7},{7,6},{8,9},{9,8},{10,11... | collective-permute-start | bytes 589832 | tf_op jit(solution)/shard_map/ppermute | solution.py:194
  96.8 1.3 collective-permute-done.3.came_b
  98.1 2.8 %collective-permute-done.2.came_a = bf16[128,768]{1,0:T(8,128)(2,1)S(1)} collective-permute-done((bf16[128,768]{1,0:T(8,128)(2,1)S(1)}, bf16[128,768]{1,0:T(8,128)(2,1)S(1)}, u32[]{:S(2)}, u32[]{:S(2)}) %collective-permute-start.2) | collective-permute-done | bytes 196640 | tf_op jit(solution)/shard_map/ppermute | solution.py:194
  100.9 0.8 shard_map.79._
  101.8 8.0 %all-to-all-start.2 = ((bf16[8,16,1536]{2,1,0:T(8,128)(2,1)}), bf16[8,16,1536]{2,1,0:T(8,128)(2,1)S(1)}, u32[]{:S(2)}, u32[]{:S(2)}) async-start(bf16[8,16,1536]{2,1,0:T(8,128)(2,1)} %bitcast.4), calls=%async_computation.2 | async-start | bytes 786432 | tf_op jit(solution)/shard_map/all_to_all | solution.py:200
  109.8 1.2 shard_map.80
  111.0 12.1 %collective-permute-start.4 = (bf16[256,768]{1,0:T(8,128)(2,1)S(1)}, bf16[256,768]{1,0:T(8,128)(2,1)S(1)}, u32[]{:S(2)}, u32[]{:S(2)}) collective-permute-start(bf16[256,768]{1,0:T(8,128)(2,1)S(1)} %get-tuple-element.24), channel_id=1, source_target_pairs={{0,16},{16,0},{1,17},{17,1},{2,18},{18,2},{3,19},{19,3},{4,20},{20... | collective-permute-start | bytes 1179656 | tf_op jit(solution)/shard_map/ppermute | solution.py:205
  123.0 1.9 %collective-permute-start.5 = (bf16[256,768]{1,0:T(8,128)(2,1)S(1)}, bf16[256,768]{1,0:T(8,128)(2,1)S(1)}, u32[]{:S(2)}, u32[]{:S(2)}) collective-permute-start(bf16[256,768]{1,0:T(8,128)(2,1)S(1)} %get-tuple-element.25), channel_id=1, source_target_pairs={{0,16},{16,0},{1,17},{17,1},{2,18},{18,2},{3,19},{19,3},{4,20},{20... | collective-permute-start | bytes 1179656 | tf_op jit(solution)/shard_map/ppermute | solution.py:205
  125.0 2.4 %collective-permute-start.6 = (bf16[256,768]{1,0:T(8,128)(2,1)S(1)}, bf16[256,768]{1,0:T(8,128)(2,1)S(1)}, u32[]{:S(2)}, u32[]{:S(2)}) collective-permute-start(bf16[256,768]{1,0:T(8,128)(2,1)S(1)} %get-tuple-element.26), channel_id=1, source_target_pairs={{0,16},{16,0},{1,17},{17,1},{2,18},{18,2},{3,19},{19,3},{4,20},{20... | collective-permute-start | bytes 1179656 | tf_op jit(solution)/shard_map/ppermute | solution.py:205
  127.4 1.9 %collective-permute-start.7 = (bf16[256,768]{1,0:T(8,128)(2,1)S(1)}, bf16[256,768]{1,0:T(8,128)(2,1)S(1)}, u32[]{:S(2)}, u32[]{:S(2)}) collective-permute-start(bf16[256,768]{1,0:T(8,128)(2,1)S(1)} %get-tuple-element.27), channel_id=1, source_target_pairs={{0,16},{16,0},{1,17},{17,1},{2,18},{18,2},{3,19},{19,3},{4,20},{20... | collective-permute-start | bytes 1179656 | tf_op jit(solution)/shard_map/ppermute | solution.py:205
  129.3 2.4 %collective-permute-start.8 = (bf16[256,768]{1,0:T(8,128)(2,1)S(1)}, bf16[256,768]{1,0:T(8,128)(2,1)S(1)}, u32[]{:S(2)}, u32[]{:S(2)}) collective-permute-start(bf16[256,768]{1,0:T(8,128)(2,1)S(1)} %get-tuple-element.28), channel_id=1, source_target_pairs={{0,16},{16,0},{1,17},{17,1},{2,18},{18,2},{3,19},{19,3},{4,20},{20... | collective-permute-start | bytes 1179656 | tf_op jit(solution)/shard_map/ppermute | solution.py:205
  131.7 0.0 collective-permute-done.4.panel2
  131.7 0.0 collective-permute-done.5.refs_0_
  131.7 0.0 collective-permute-done.6.refs_1_
  131.8 0.0 collective-permute-done.7.refs_2_
  131.8 1.3 collective-permute-done.8.refs_3_
  133.1 3.0 %shard_map.81 = (bf16[384,1536]{1,0:T(8,128)(2,1)}, bf16[1536,384]{1,0:T(8,128)(2,1)}) custom-call(bf16[256,1536]{1,0:T(8,128)(2,1)S(1)} %all_gather.10.panel, bf16[256,768]{1,0:T(8,128)(2,1)S(1)} %collective-permute-done.4.panel2, bf16[256,3072]{1,0:T(8,128)(2,1)S(1)} %bitcast.9, bf16[256,768]{1,0:T(8,128)(2,1)S(1)} %collective-permute-done.5.refs_0_, ...), custom_call_target="tpu_custom_call" | custom-call | flops 1207959552 | bytes 6684672 | tf_op jit(solution)/shard_map/pallas_call | solution.py:42
  136.1 0.0 all-to-all-done.2
  136.1 0.1 shard_map.82
  136.1 3.8 %all_gather.11.both = bf16[32,1536]{1,0:T(8,128)(2,1)S(1)} all-gather(bf16[16,1536]{1,0:T(8,128)(2,1)S(1)} %shard_map.82), channel_id=1, replica_groups=mesh['y'=4,'x'=4,'core'=2,'zh'=8,'zl'=2] {'core'}, dimensions={0}, use_global_device_ids=true | all-gather | bytes 147456 | tf_op jit(solution)/shard_map/all_gather | solution.py:218
  139.9 1.2 shard_map.83
  (2 shorter events, 0.0 us)
Async XLA Ops:
  0.6 42.0 %copy-start = (bf16[384,1536]{1,0:T(8,128)(2,1)S(1)}, bf16[384,1536]{1,0:T(8,128)(2,1)}, u32[]{:S(2)}) copy-start(bf16[384,1536]{1,0:T(8,128)(2,1)} %up.3) | copy-start | bytes 3538948
  0.6 42.0 %collective-permute-start = (bf16[384,1536]{1,0:T(8,128)(2,1)}, bf16[384,1536]{1,0:T(8,128)(2,1)}, u32[]{:S(2)}, u32[]{:S(2)}) collective-permute-start(bf16[384,1536]{1,0:T(8,128)(2,1)} %up.3), channel_id=1, source_target_pairs={{0,16},{16,0},{1,17},{17,1},{2,18},{18,2},{3,19},{19,3},{4,20},{20... | collective-permute-start | bytes 3538952 | tf_op jit(solution)/shard_map/ppermute | solution.py:168
  9.6 33.0 %collective-permute-start.1 = (bf16[1536,384]{1,0:T(8,128)(2,1)}, bf16[1536,384]{1,0:T(8,128)(2,1)S(1)}, u32[]{:S(2)}, u32[]{:S(2)}) collective-permute-start(bf16[1536,384]{1,0:T(8,128)(2,1)} %down.3), channel_id=1, source_target_pairs={{0,16},{16,0},{1,17},{17,1},{2,18},{18,2},{3,19},{19,3},{4,20},{20... | collective-permute-start | bytes 3538952 | tf_op jit(solution)/shard_map/ppermute | solution.py:169
  42.6 1.3 copy-start.1
  43.9 3.5 %copy-start.3 = (bf16[1536,384]{1,0:T(8,128)(2,1)}, bf16[1536,384]{1,0:T(8,128)(2,1)S(1)}, u32[]{:S(2)}) copy-start(bf16[1536,384]{1,0:T(8,128)(2,1)S(1)} %collective-permute-done.1.down2) | copy-start | bytes 3538948
  88.1 4.9 %copy-start.2 = (bf16[1536,384]{1,0:T(8,128)(2,1)S(1)}, bf16[1536,384]{1,0:T(8,128)(2,1)}, u32[]{:S(2)}) copy-start(bf16[1536,384]{1,0:T(8,128)(2,1)} %down.3) | copy-start | bytes 3538948
  88.1 4.9 %copy-start.4 = (bf16[1536,384]{1,0:T(8,128)(2,1)S(1)}, bf16[1536,384]{1,0:T(8,128)(2,1)}, u32[]{:S(2)}) copy-start(bf16[1536,384]{1,0:T(8,128)(2,1)} %copy-done.3) | copy-start | bytes 3538948
  90.5 7.6 %collective-permute-start.3 = (bf16[128,768]{1,0:T(8,128)(2,1)S(1)}, bf16[128,768]{1,0:T(8,128)(2,1)S(1)}, u32[]{:S(2)}, u32[]{:S(2)}) collective-permute-start(bf16[128,768]{1,0:T(8,128)(2,1)S(1)} %get-tuple-element.23), channel_id=1, source_target_pairs={{0,15},{1,2},{2,1},{3,4},{4,3},{5,6},{6,5},{7,8},{8,7},{9,10},{10,... | collective-permute-start | bytes 589832 | tf_op jit(solution)/shard_map/ppermute | solution.py:196
  94.5 6.4 %collective-permute-start.2 = (bf16[128,768]{1,0:T(8,128)(2,1)S(1)}, bf16[128,768]{1,0:T(8,128)(2,1)S(1)}, u32[]{:S(2)}, u32[]{:S(2)}) collective-permute-start(bf16[128,768]{1,0:T(8,128)(2,1)S(1)} %get-tuple-element.21), channel_id=1, source_target_pairs={{0,1},{1,0},{2,3},{3,2},{4,5},{5,4},{6,7},{7,6},{8,9},{9,8},{10,11... | collective-permute-start | bytes 589832 | tf_op jit(solution)/shard_map/ppermute | solution.py:194
  101.8 34.3 %all-to-all-start.2 = ((bf16[8,16,1536]{2,1,0:T(8,128)(2,1)}), bf16[8,16,1536]{2,1,0:T(8,128)(2,1)S(1)}, u32[]{:S(2)}, u32[]{:S(2)}) async-start(bf16[8,16,1536]{2,1,0:T(8,128)(2,1)} %bitcast.4), calls=%async_computation.2 | async-start | bytes 786432 | tf_op jit(solution)/shard_map/all_to_all | solution.py:200
  111.0 20.8 %collective-permute-start.4 = (bf16[256,768]{1,0:T(8,128)(2,1)S(1)}, bf16[256,768]{1,0:T(8,128)(2,1)S(1)}, u32[]{:S(2)}, u32[]{:S(2)}) collective-permute-start(bf16[256,768]{1,0:T(8,128)(2,1)S(1)} %get-tuple-element.24), channel_id=1, source_target_pairs={{0,16},{16,0},{1,17},{17,1},{2,18},{18,2},{3,19},{19,3},{4,20},{20... | collective-permute-start | bytes 1179656 | tf_op jit(solution)/shard_map/ppermute | solution.py:205
  123.0 8.7 %collective-permute-start.5 = (bf16[256,768]{1,0:T(8,128)(2,1)S(1)}, bf16[256,768]{1,0:T(8,128)(2,1)S(1)}, u32[]{:S(2)}, u32[]{:S(2)}) collective-permute-start(bf16[256,768]{1,0:T(8,128)(2,1)S(1)} %get-tuple-element.25), channel_id=1, source_target_pairs={{0,16},{16,0},{1,17},{17,1},{2,18},{18,2},{3,19},{19,3},{4,20},{20... | collective-permute-start | bytes 1179656 | tf_op jit(solution)/shard_map/ppermute | solution.py:205
  125.0 6.8 %collective-permute-start.6 = (bf16[256,768]{1,0:T(8,128)(2,1)S(1)}, bf16[256,768]{1,0:T(8,128)(2,1)S(1)}, u32[]{:S(2)}, u32[]{:S(2)}) collective-permute-start(bf16[256,768]{1,0:T(8,128)(2,1)S(1)} %get-tuple-element.26), channel_id=1, source_target_pairs={{0,16},{16,0},{1,17},{17,1},{2,18},{18,2},{3,19},{19,3},{4,20},{20... | collective-permute-start | bytes 1179656 | tf_op jit(solution)/shard_map/ppermute | solution.py:205
  127.4 4.4 %collective-permute-start.7 = (bf16[256,768]{1,0:T(8,128)(2,1)S(1)}, bf16[256,768]{1,0:T(8,128)(2,1)S(1)}, u32[]{:S(2)}, u32[]{:S(2)}) collective-permute-start(bf16[256,768]{1,0:T(8,128)(2,1)S(1)} %get-tuple-element.27), channel_id=1, source_target_pairs={{0,16},{16,0},{1,17},{17,1},{2,18},{18,2},{3,19},{19,3},{4,20},{20... | collective-permute-start | bytes 1179656 | tf_op jit(solution)/shard_map/ppermute | solution.py:205
  129.3 3.7 %collective-permute-start.8 = (bf16[256,768]{1,0:T(8,128)(2,1)S(1)}, bf16[256,768]{1,0:T(8,128)(2,1)S(1)}, u32[]{:S(2)}, u32[]{:S(2)}) collective-permute-start(bf16[256,768]{1,0:T(8,128)(2,1)S(1)} %get-tuple-element.28), channel_id=1, source_target_pairs={{0,16},{16,0},{1,17},{17,1},{2,18},{18,2},{3,19},{19,3},{4,20},{20... | collective-permute-start | bytes 1179656 | tf_op jit(solution)/shard_map/ppermute | solution.py:205

commit v3 on v2

v3 whole, which is shorter than its diff:
```python
import functools
import math

import jax
import jax.numpy as jnp
from jax import lax
from jax.experimental import pallas as pl
from jax.experimental.pallas import tpu as pltpu
from jax.sharding import Mesh
from jax.sharding import PartitionSpec as P

BF16 = jnp.bfloat16
F32 = jnp.float32
COEF = math.sqrt(2.0 / math.pi)
PLANE = ("y", "x")
COL = ("zh", "zl")
SWAP = [(0, 1), (1, 0)]
EVEN = [(z, z ^ 1) for z in range(16)]
ODD = [(z, (((z - 1) ^ 1) + 1) % 16) for z in range(16)]
TILE = 256
PIECES = 3
MIB = 1024 * 1024
VMEM = pl.BlockSpec(memory_space=pltpu.VMEM)
SMEM = pl.BlockSpec(memory_space=pltpu.SMEM)


def gelu_and_slope(z):
    t = jnp.tanh(COEF * (z + 0.044715 * z * z * z))
    value = 0.5 * z * (1.0 + t)
    slope = 0.5 * (1.0 + t) + 0.5 * z * (1.0 - t * t) * COEF * (1.0 + 3.0 * 0.044715 * z * z)
    return value, slope


def matmul(a, b, left, right):
    return lax.dot_general(a, b, (((left,), (right,)), ((), ())), preferred_element_type=F32)


def call(kernel, out_shape, flops, *args, scratch=()):
    specs = [SMEM if a.dtype == jnp.int32 else VMEM for a in args]
    size = sum(a.size * a.dtype.itemsize for a in args) + sum(
        math.prod(o.shape) * o.dtype.itemsize for o in out_shape
    )
    return pl.pallas_call(
        kernel,
        out_shape=out_shape,
        in_specs=specs,
        out_specs=[VMEM] * len(out_shape),
        scratch_shapes=scratch,
        compiler_params=pltpu.CompilerParams(vmem_limit_bytes=10 * MIB),
        cost_estimate=pl.CostEstimate(flops=flops, bytes_accessed=size, transcendentals=0),
    )(*args)


def shape(*dims):
    return jax.ShapeDtypeStruct(dims, BF16)


def pick_kernel(core_ref, _, pair, out):
    part = out.shape[0]
    rows, cols = 2 * part, pair.shape[1]
    core = core_ref[0]
    mine = pl.multiple_of(core * rows + core * part, part)
    theirs = pl.multiple_of((1 - core) * rows + core * part, part)
    out[:, :cols] = pair[pl.ds(mine, part), :]
    out[:, cols:] = pair[pl.ds(theirs, part), :]


def first_kernel(panel, up, down, up2, down2, out):
    width, hid = up.shape
    act, cot, act2, cot2 = [panel[:, q * width : (q + 1) * width] for q in range(4)]
    for t in range(0, hid, TILE):
        span = slice(t, t + TILE)
        out[:, span] = (
            matmul(act, up[:, span], 1, 0) + matmul(act2, up2[:, span], 1, 0)
        ).astype(BF16)
        out[:, hid + t : hid + t + TILE] = (
            matmul(cot, down[span, :], 1, 1) + matmul(cot2, down2[span, :], 1, 1)
        ).astype(BF16)


def middle_kernel(got, spread):
    members = 16
    part = got.shape[0] // members
    hid = got.shape[1] // 2

    def summed(cols):
        total = got[:part, cols].astype(F32)
        for q in range(1, members):
            total = total + got[q * part : (q + 1) * part, cols].astype(F32)
        return total

    for t in range(0, hid, TILE):
        here, there = slice(t, t + TILE), slice(hid + t, hid + t + TILE)
        value, slope = gelu_and_slope(summed(here))
        value = value.astype(BF16)
        slope = (summed(there) * slope).astype(BF16)
        for q in range(members):
            spread[q * part : (q + 1) * part, here] = value
            spread[q * part : (q + 1) * part, there] = slope


def second_kernel(flip, zl_ref, block, up, down, up2, down2, output, grad_input, rows):
    width, hid = up.shape
    part = 16
    parity = 1 - zl_ref[0] if flip else zl_ref[0]
    for q in range(rows.shape[0] // part):
        begin = pl.multiple_of((2 * q + parity) * part, part)
        rows[q * part : (q + 1) * part, :] = block[pl.ds(begin, part), :]
    output[:, :width] = matmul(rows[:, :hid], down[...], 1, 0).astype(BF16)
    output[:, width:] = matmul(rows[:, :hid], down2[...], 1, 0).astype(BF16)
    grad_input[:, :width] = matmul(rows[:, hid:], up[...], 1, 1).astype(BF16)
    grad_input[:, width:] = matmul(rows[:, hid:], up2[...], 1, 1).astype(BF16)


def pair_kernel(keep_a, came_a, keep_b, came_b, out):
    cols = keep_a.shape[1]
    out[:, :cols] = (keep_a[...].astype(F32) + came_a[...].astype(F32)).astype(BF16)
    out[:, cols:] = (keep_b[...].astype(F32) + came_b[...].astype(F32)).astype(BF16)


def stage_kernel(_, own, panel, *outs):
    cols = outs[0].shape[1]
    split = own.shape[1]
    for q, out in enumerate(outs):
        begin, end = q * cols, (q + 1) * cols
        if end <= split:
            out[...] = own[:, begin:end]
        else:
            rest = panel.shape[1] // 2 + begin - split
            if begin < split:
                out[:, : split - begin] = own[:, begin:]
                rest = panel.shape[1] // 2
            out[:, max(split - begin, 0) :] = panel[:, rest : rest + end - max(split, begin)]


def sum_kernel(parts, out):
    rows = out.shape[0]
    total = parts[:rows, :].astype(F32)
    for q in range(1, parts.shape[0] // rows):
        total = total + parts[q * rows : (q + 1) * rows, :].astype(F32)
    out[...] = total.astype(BF16)


def last_kernel(core_ref, both, output, grad_input):
    rows, width = output.shape
    part = rows // 2
    core = core_ref[0]
    for source in range(2):
        place = slice(source * part, (source + 1) * part)
        own = core == source
        output[place, :] = jnp.where(own, both[place, :width], both[place, width : 2 * width])
        grad_input[place, :] = jnp.where(
            own, both[place, 2 * width : 3 * width], both[place, 3 * width :]
        )


def grads_kernel(panel, own, *refs):
    *others, grad_up, grad_down = refs
    width, hid = grad_up.shape
    piece = others[0].shape[1]

    def other(begin, size):
        return others[begin // piece][:, begin % piece : begin % piece + size]

    act, cot = panel[:, :width], panel[:, width : 2 * width]
    act2, cot2 = other(2 * hid, width), other(2 * hid + width, width)
    for j in range(0, hid, TILE):
        grad_down[j : j + TILE, :] = (
            matmul(own[:, j : j + TILE], cot, 0, 0) + matmul(other(j, TILE), cot2, 0, 0)
        ).astype(BF16)
        grad_up[:, j : j + TILE] = (
            matmul(act, own[:, hid + j : hid + j + TILE], 0, 0)
            + matmul(act2, other(hid + j, TILE), 0, 0)
        ).astype(BF16)


def per_device(activations, up, down, cotangent):
    rows, width = activations.shape
    hid = up.shape[1]
    core = lax.axis_index("core").astype(jnp.int32).reshape(1)
    zl = lax.axis_index("zl").astype(jnp.int32).reshape(1)
    part = rows // 2
    half = 16 * part
    members = 16
    work = 8 * half * width * hid

    up2 = lax.ppermute(up, "core", SWAP)
    down2 = lax.ppermute(down, "core", SWAP)
    pair = lax.all_gather(
        jnp.concatenate([activations, cotangent], axis=1), "core", axis=0, tiled=True
    )
    (mine,) = call(pick_kernel, [shape(part, 4 * width)], 8 * work, core, zl, pair)
    panel = lax.all_gather(mine, COL, axis=0, tiled=True)

    (partial,) = call(
        first_kernel, [shape(half, 2 * hid)], work, panel, up, down, up2, down2
    )

    got = lax.all_to_all(partial, PLANE, 0, 0, tiled=True)
    (spread,) = call(middle_kernel, [shape(half, 2 * hid)], 8 * work, got)
    own = lax.all_to_all(spread, PLANE, 0, 0, tiled=True)

    def second(flip):
        return call(
            functools.partial(second_kernel, flip),
            [shape(half // 2, 2 * width)] * 2,
            work // 2,
            zl,
            own,
            up,
            down,
            up2,
            down2,
            scratch=[pltpu.VMEM((half // 2, 2 * hid), BF16)],
        )

    send_out, send_in = second(True)
    came_out = lax.ppermute(send_out, COL, EVEN)
    came_in = lax.ppermute(send_in, COL, ODD)
    keep_out, keep_in = second(False)
    (added,) = call(
        pair_kernel, [shape(half // 2, 4 * width)], 0, keep_out, came_out, keep_in, came_in
    )
    gathered = lax.all_to_all(added, "zh", 0, 0, tiled=True)

    piece = (2 * hid + 2 * width) // PIECES
    pieces = call(stage_kernel, [shape(half, piece)] * PIECES, work // 4, added, own, panel)
    others = [lax.ppermute(piece, "core", SWAP) for piece in pieces]
    grad_up, grad_down = call(
        grads_kernel, [shape(width, hid), shape(hid, width)], work, panel, own, *others
    )

    gathered, grad_up, grad_down = lax.optimization_barrier((gathered, grad_up, grad_down))
    (summed,) = call(sum_kernel, [shape(part, 4 * width)], 0, gathered)
    both = lax.all_gather(summed, "core", axis=0, tiled=True)
    output, grad_input = call(last_kernel, [shape(rows, width)] * 2, 0, core, both)
    return (output, grad_input, grad_up, grad_down)


def solution(mesh):
    fine = Mesh(mesh.devices.reshape(4, 4, 2, 8, 2), ("y", "x", "core", "zh", "zl"))
    row = ("y", "x", "core")
    return jax.shard_map(
        per_device,
        mesh=fine,
        in_specs=(P(COL, row), P(row, COL), P(COL, row), P(COL, row)),
        out_specs=(P(COL, row), P(COL, row), P(row, COL), P(COL, row)),
        check_vma=False,
    )
```

time: 142 us -> 134 us (0.944)
  Pallas kernels: 14.3 us -> 10.3 us
  starting transfers between devices: 44.3 us -> 40.5 us
  blocking collectives: 73.6 us -> 77.1 us
  local copies, waits for them, and re-layouts: 1.45 us -> 0.02 us
    pallas_call x9 -> x10, Pallas kernels: 14.3 us -> 10.3 us  [call(): pl.pallas_call(kernel, out_shape=out_shape, in_specs=specs, out_specs=[VM...]
    ppermute x5 -> x3, starting transfers between devices: 20.7 us -> 16.8 us  [per_device(): others = [lax.ppermute(piece, 'core', SWAP) for piece in pieces]]
    all_gather x1, blocking collectives: 3.77 us -> 6.93 us  [per_device(): both = lax.all_gather(summed, 'core', axis=0, tiled=True)]
    ppermute x1, waiting for transfers between devices: 2.8 us -> 0.01 us  [per_device(): came_out = lax.ppermute(send_out, COL, EVEN)]
    ppermute x1, starting transfers between devices: 2.42 us -> 4.02 us  [per_device(): came_in = lax.ppermute(send_in, COL, ODD)]
  transfers between devices with their start and end apart: 10 -> 8, of which waited for: 3 -> 2; matrix products, arithmetic and copies ran while one was open for 1% -> 1% of each run, Pallas kernels for 4% -> 4%
where the time goes in v3:
time: 134 us
  blocking collectives  77.1 us (58%)
  starting transfers between devices  40.5 us (30%)
  Pallas kernels  10.3 us (8%)
  waiting for transfers between devices  4.05 us (3%)
    all_gather x1, blocking collectives, per_device(): panel = lax.all_gather(mine, COL, axis=0, tiled=True)  27.7 us
    all_to_all x1, blocking collectives, per_device(): got = lax.all_to_all(partial, PLANE, 0, 0, tiled=True)  22.4 us
    all_to_all x1, blocking collectives, per_device(): own = lax.all_to_all(spread, PLANE, 0, 0, tiled=True)  17.9 us
    ppermute x3, starting transfers between devices, per_device(): others = [lax.ppermute(piece, 'core', SWAP) for piece in pieces]  16.8 us
    pallas_call x10, Pallas kernels, call(): pl.pallas_call(kernel, out_shape=out_shape, in_specs=specs, out_specs=[VM...  10.3 us
    ppermute x1, starting transfers between devices, per_device(): up2 = lax.ppermute(up, 'core', SWAP)  8.79 us
    all_to_all x1, starting transfers between devices, per_device(): gathered = lax.all_to_all(added, 'zh', 0, 0, tiled=True)  7.12 us
    all_gather x1, blocking collectives, per_device(): both = lax.all_gather(summed, 'core', axis=0, tiled=True)  6.93 us
  transfers between devices with their start and end apart: 8, of which 2 were waited for; matrix products, arithmetic and copies ran while one was open for 1% of the time, Pallas kernels for 4%

profile of v3, /device:TPU:1, one launch (start us, length us, event | category | flops | bytes accessed | tf_op | source)
XLA Modules:
  0.0 133.5 jit_solution(7270294575103218225)
XLA Ops:
  0.6 8.8 %collective-permute-start = (bf16[384,1536]{1,0:T(8,128)(2,1)}, bf16[384,1536]{1,0:T(8,128)(2,1)S(1)}, u32[]{:S(2)}, u32[]{:S(2)}) collective-permute-start(bf16[384,1536]{1,0:T(8,128)(2,1)} %up.5), channel_id=1, source_target_pairs={{0,16},{16,0},{1,17},{17,1},{2,18},{18,2},{3,19},{19,3},{4,20},{20... | collective-permute-start | bytes 3538952 | tf_op jit(solution)/shard_map/ppermute | solution.py:187
  9.4 1.9 %collective-permute-start.1 = (bf16[1536,384]{1,0:T(8,128)(2,1)}, bf16[1536,384]{1,0:T(8,128)(2,1)S(1)}, u32[]{:S(2)}, u32[]{:S(2)}) collective-permute-start(bf16[1536,384]{1,0:T(8,128)(2,1)} %down.5), channel_id=1, source_target_pairs={{0,16},{16,0},{1,17},{17,1},{2,18},{18,2},{3,19},{19,3},{4,20},{20... | collective-permute-start | bytes 3538952 | tf_op jit(solution)/shard_map/ppermute | solution.py:188
  11.4 0.8 pad_maximum_fusion
  12.1 2.1 %all_gather.9.pair = bf16[64,768]{1,0:T(8,128)(2,1)S(1)} all-gather(bf16[32,768]{1,0:T(8,128)(2,1)S(1)} %pad_maximum_fusion), channel_id=1, replica_groups=mesh['y'=4,'x'=4,'core'=2,'zh'=8,'zl'=2] {'core'}, dimensions={0}, use_global_device_ids=true | all-gather | bytes 147456 | tf_op jit(solution)/shard_map/all_gather | solution.py:189
  14.2 0.0 copy-start
  14.2 0.0 copy-start.1
  14.3 27.7 %all_gather.10.panel = bf16[256,1536]{1,0:T(8,128)(2,1)S(1)} all-gather(bf16[16,1536]{1,0:T(8,128)(2,1)S(1)} %shard_map.75), channel_id=1, replica_groups=mesh['y'=4,'x'=4,'core'=2,'zh'=8,'zl'=2] {'zh','zl'}, dimensions={0}, use_global_device_ids=true | all-gather | bytes 835584 | tf_op jit(solution)/shard_map/all_gather | solution.py:193
  42.0 0.0 collective-permute-done.up2
  42.0 0.0 collective-permute-done.1.down2
  42.0 0.0 copy-done
  42.0 0.0 copy-done.1
  42.0 0.0 copy-start.2
  42.0 1.8 %shard_map.76 = bf16[256,3072]{1,0:T(8,128)(2,1)S(1)} custom-call(bf16[256,1536]{1,0:T(8,128)(2,1)S(1)} %all_gather.10.panel, bf16[384,1536]{1,0:T(8,128)(2,1)S(1)} %copy-done, bf16[1536,384]{1,0:T(8,128)(2,1)S(1)} %copy-done.1, bf16[384,1536]{1,0:T(8,128)(2,1)S(1)} %collective-permute-done.up2, bf16[1536,384]{1,0:T(8,128)(2,1)S(1)} %collective-permute-done.1.down2), custom_call_target="tpu_custom_call" | custom-call | flops 1207959552 | bytes 7077888 | tf_op jit(solution)/shard_map/pallas_call | solution.py:43
  43.8 0.0 copy-done.2
  43.8 22.4 %all_to_all.34 = bf16[16,16,3072]{2,1,0:T(8,128)(2,1)S(1)} all-to-all(bf16[16,16,3072]{2,1,0:T(8,128)(2,1)S(1)} %bitcast.12), channel_id=1, replica_groups=mesh['y'=4,'x'=4,'core'=2,'zh'=8,'zl'=2] {'y','x'}, dimensions={0} | all-to-all | bytes 3145728 | tf_op jit(solution)/shard_map/all_to_all | solution.py:199
  66.2 0.3 shard_map.77
  66.5 0.0 copy-start.3
  66.5 17.9 %all_to_all.35 = bf16[16,16,3072]{2,1,0:T(8,128)(2,1)S(1)} all-to-all(bf16[16,16,3072]{2,1,0:T(8,128)(2,1)S(1)} %bitcast.14), channel_id=1, replica_groups=mesh['y'=4,'x'=4,'core'=2,'zh'=8,'zl'=2] {'y','x'}, dimensions={0} | all-to-all | bytes 3145728 | tf_op jit(solution)/shard_map/all_to_all | solution.py:201
  84.5 0.0 copy-done.3
  84.5 1.2 shard_map.79
  85.7 1.9 %collective-permute-start.2 = (bf16[128,768]{1,0:T(8,128)(2,1)S(1)}, bf16[128,768]{1,0:T(8,128)(2,1)S(1)}, u32[]{:S(2)}, u32[]{:S(2)}) collective-permute-start(bf16[128,768]{1,0:T(8,128)(2,1)S(1)} %get-tuple-element.19), channel_id=1, source_target_pairs={{0,1},{1,0},{2,3},{3,2},{4,5},{5,4},{6,7},{7,6},{8,9},{9,8},{10,11... | collective-permute-start | bytes 589832 | tf_op jit(solution)/shard_map/ppermute | solution.py:218
  87.6 4.0 %collective-permute-start.3 = (bf16[128,768]{1,0:T(8,128)(2,1)S(1)}, bf16[128,768]{1,0:T(8,128)(2,1)S(1)}, u32[]{:S(2)}, u32[]{:S(2)}) collective-permute-start(bf16[128,768]{1,0:T(8,128)(2,1)S(1)} %get-tuple-element.21), channel_id=1, source_target_pairs={{0,15},{1,2},{2,1},{3,4},{4,3},{5,6},{6,5},{7,8},{8,7},{9,10},{10,... | collective-permute-start | bytes 589832 | tf_op jit(solution)/shard_map/ppermute | solution.py:219
  91.7 1.2 shard_map.78
  92.9 0.0 collective-permute-done.2.came_a
  92.9 2.4 %collective-permute-done.3.came_b = bf16[128,768]{1,0:T(8,128)(2,1)S(1)} collective-permute-done((bf16[128,768]{1,0:T(8,128)(2,1)S(1)}, bf16[128,768]{1,0:T(8,128)(2,1)S(1)}, u32[]{:S(2)}, u32[]{:S(2)}) %collective-permute-start.3) | collective-permute-done | bytes 196640 | tf_op jit(solution)/shard_map/ppermute | solution.py:219
  95.3 0.9 shard_map.80._
  96.1 7.1 %all-to-all-start.2 = ((bf16[8,16,1536]{2,1,0:T(8,128)(2,1)}), bf16[8,16,1536]{2,1,0:T(8,128)(2,1)S(1)}, u32[]{:S(2)}, u32[]{:S(2)}) async-start(bf16[8,16,1536]{2,1,0:T(8,128)(2,1)} %bitcast.6), calls=%async_computation.2 | async-start | bytes 786432 | tf_op jit(solution)/shard_map/all_to_all | solution.py:224
  103.2 1.2 shard_map.81
  104.4 12.4 %collective-permute-start.4 = (bf16[256,1280]{1,0:T(8,128)(2,1)S(1)}, bf16[256,1280]{1,0:T(8,128)(2,1)S(1)}, u32[]{:S(2)}, u32[]{:S(2)}) collective-permute-start(bf16[256,1280]{1,0:T(8,128)(2,1)S(1)} %get-tuple-element.22), channel_id=1, source_target_pairs={{0,16},{16,0},{1,17},{17,1},{2,18},{18,2},{3,19},{19,3},{4,20},{20... | collective-permute-start | bytes 1966088 | tf_op jit(solution)/shard_map/ppermute | solution.py:228
  116.8 1.9 %collective-permute-start.5 = (bf16[256,1280]{1,0:T(8,128)(2,1)S(1)}, bf16[256,1280]{1,0:T(8,128)(2,1)S(1)}, u32[]{:S(2)}, u32[]{:S(2)}) collective-permute-start(bf16[256,1280]{1,0:T(8,128)(2,1)S(1)} %get-tuple-element.23), channel_id=1, source_target_pairs={{0,16},{16,0},{1,17},{17,1},{2,18},{18,2},{3,19},{19,3},{4,20},{20... | collective-permute-start | bytes 1966088 | tf_op jit(solution)/shard_map/ppermute | solution.py:228
  118.8 2.4 %collective-permute-start.6 = (bf16[256,1280]{1,0:T(8,128)(2,1)S(1)}, bf16[256,1280]{1,0:T(8,128)(2,1)S(1)}, u32[]{:S(2)}, u32[]{:S(2)}) collective-permute-start(bf16[256,1280]{1,0:T(8,128)(2,1)S(1)} %get-tuple-element.24), channel_id=1, source_target_pairs={{0,16},{16,0},{1,17},{17,1},{2,18},{18,2},{3,19},{19,3},{4,20},{20... | collective-permute-start | bytes 1966088 | tf_op jit(solution)/shard_map/ppermute | solution.py:228
  121.2 0.0 collective-permute-done.4.refs_0_
  121.2 0.0 collective-permute-done.5.refs_1_
  121.2 1.7 %collective-permute-done.6.refs_2_ = bf16[256,1280]{1,0:T(8,128)(2,1)S(1)} collective-permute-done((bf16[256,1280]{1,0:T(8,128)(2,1)S(1)}, bf16[256,1280]{1,0:T(8,128)(2,1)S(1)}, u32[]{:S(2)}, u32[]{:S(2)}) %collective-permute-start.6) | collective-permute-done | bytes 655392 | tf_op jit(solution)/shard_map/ppermute | solution.py:228
  122.9 3.0 %shard_map.82 = (bf16[384,1536]{1,0:T(8,128)(2,1)}, bf16[1536,384]{1,0:T(8,128)(2,1)}) custom-call(bf16[256,1536]{1,0:T(8,128)(2,1)S(1)} %all_gather.10.panel, bf16[256,3072]{1,0:T(8,128)(2,1)S(1)} %bitcast.11, bf16[256,1280]{1,0:T(8,128)(2,1)S(1)} %collective-permute-done.4.refs_0_, bf16[256,1280]{1,0:T(8,128)(2,1)S(1)} %collective-permute-done.5.refs_1_, ...), custom_call_target="tpu_custom_call" | custom-call | flops 1207959552 | bytes 6684672 | tf_op jit(solution)/shard_map/pallas_call | solution.py:43
  125.9 0.0 all-to-all-done.2
  125.9 0.1 shard_map.83
  126.0 6.9 %all_gather.11.both = bf16[32,1536]{1,0:T(8,128)(2,1)S(1)} all-gather(bf16[16,1536]{1,0:T(8,128)(2,1)S(1)} %shard_map.83), channel_id=1, replica_groups=mesh['y'=4,'x'=4,'core'=2,'zh'=8,'zl'=2] {'core'}, dimensions={0}, use_global_device_ids=true | all-gather | bytes 147456 | tf_op jit(solution)/shard_map/all_gather | solution.py:235
  132.9 0.6 shard_map.84
  (1 shorter events, 0.0 us)
Async XLA Ops:
  0.6 41.4 %collective-permute-start = (bf16[384,1536]{1,0:T(8,128)(2,1)}, bf16[384,1536]{1,0:T(8,128)(2,1)S(1)}, u32[]{:S(2)}, u32[]{:S(2)}) collective-permute-start(bf16[384,1536]{1,0:T(8,128)(2,1)} %up.5), channel_id=1, source_target_pairs={{0,16},{16,0},{1,17},{17,1},{2,18},{18,2},{3,19},{19,3},{4,20},{20... | collective-permute-start | bytes 3538952 | tf_op jit(solution)/shard_map/ppermute | solution.py:187
  9.4 32.6 %collective-permute-start.1 = (bf16[1536,384]{1,0:T(8,128)(2,1)}, bf16[1536,384]{1,0:T(8,128)(2,1)S(1)}, u32[]{:S(2)}, u32[]{:S(2)}) collective-permute-start(bf16[1536,384]{1,0:T(8,128)(2,1)} %down.5), channel_id=1, source_target_pairs={{0,16},{16,0},{1,17},{17,1},{2,18},{18,2},{3,19},{19,3},{4,20},{20... | collective-permute-start | bytes 3538952 | tf_op jit(solution)/shard_map/ppermute | solution.py:188
  14.2 27.7 %copy-start = (bf16[384,1536]{1,0:T(8,128)(2,1)S(1)}, bf16[384,1536]{1,0:T(8,128)(2,1)}, u32[]{:S(2)}) copy-start(bf16[384,1536]{1,0:T(8,128)(2,1)} %up.5) | copy-start | bytes 3538948
  14.2 27.7 %copy-start.1 = (bf16[1536,384]{1,0:T(8,128)(2,1)S(1)}, bf16[1536,384]{1,0:T(8,128)(2,1)}, u32[]{:S(2)}) copy-start(bf16[1536,384]{1,0:T(8,128)(2,1)} %down.5) | copy-start | bytes 3538948
  42.0 1.8 %copy-start.2 = (bf16[1536,384]{1,0:T(8,128)(2,1)}, bf16[1536,384]{1,0:T(8,128)(2,1)S(1)}, u32[]{:S(2)}) copy-start(bf16[1536,384]{1,0:T(8,128)(2,1)S(1)} %collective-permute-done.1.down2) | copy-start | bytes 3538948
  66.5 18.0 %copy-start.3 = (bf16[1536,384]{1,0:T(8,128)(2,1)S(1)}, bf16[1536,384]{1,0:T(8,128)(2,1)}, u32[]{:S(2)}) copy-start(bf16[1536,384]{1,0:T(8,128)(2,1)} %copy-done.2) | copy-start | bytes 3538948
  85.7 7.2 %collective-permute-start.2 = (bf16[128,768]{1,0:T(8,128)(2,1)S(1)}, bf16[128,768]{1,0:T(8,128)(2,1)S(1)}, u32[]{:S(2)}, u32[]{:S(2)}) collective-permute-start(bf16[128,768]{1,0:T(8,128)(2,1)S(1)} %get-tuple-element.19), channel_id=1, source_target_pairs={{0,1},{1,0},{2,3},{3,2},{4,5},{5,4},{6,7},{7,6},{8,9},{9,8},{10,11... | collective-permute-start | bytes 589832 | tf_op jit(solution)/shard_map/ppermute | solution.py:218
  87.6 7.6 %collective-permute-start.3 = (bf16[128,768]{1,0:T(8,128)(2,1)S(1)}, bf16[128,768]{1,0:T(8,128)(2,1)S(1)}, u32[]{:S(2)}, u32[]{:S(2)}) collective-permute-start(bf16[128,768]{1,0:T(8,128)(2,1)S(1)} %get-tuple-element.21), channel_id=1, source_target_pairs={{0,15},{1,2},{2,1},{3,4},{4,3},{5,6},{6,5},{7,8},{8,7},{9,10},{10,... | collective-permute-start | bytes 589832 | tf_op jit(solution)/shard_map/ppermute | solution.py:219
  96.1 29.8 %all-to-all-start.2 = ((bf16[8,16,1536]{2,1,0:T(8,128)(2,1)}), bf16[8,16,1536]{2,1,0:T(8,128)(2,1)S(1)}, u32[]{:S(2)}, u32[]{:S(2)}) async-start(bf16[8,16,1536]{2,1,0:T(8,128)(2,1)} %bitcast.6), calls=%async_computation.2 | async-start | bytes 786432 | tf_op jit(solution)/shard_map/all_to_all | solution.py:224
  104.4 16.8 %collective-permute-start.4 = (bf16[256,1280]{1,0:T(8,128)(2,1)S(1)}, bf16[256,1280]{1,0:T(8,128)(2,1)S(1)}, u32[]{:S(2)}, u32[]{:S(2)}) collective-permute-start(bf16[256,1280]{1,0:T(8,128)(2,1)S(1)} %get-tuple-element.22), channel_id=1, source_target_pairs={{0,16},{16,0},{1,17},{17,1},{2,18},{18,2},{3,19},{19,3},{4,20},{20... | collective-permute-start | bytes 1966088 | tf_op jit(solution)/shard_map/ppermute | solution.py:228
  116.8 4.4 %collective-permute-start.5 = (bf16[256,1280]{1,0:T(8,128)(2,1)S(1)}, bf16[256,1280]{1,0:T(8,128)(2,1)S(1)}, u32[]{:S(2)}, u32[]{:S(2)}) collective-permute-start(bf16[256,1280]{1,0:T(8,128)(2,1)S(1)} %get-tuple-element.23), channel_id=1, source_target_pairs={{0,16},{16,0},{1,17},{17,1},{2,18},{18,2},{3,19},{19,3},{4,20},{20... | collective-permute-start | bytes 1966088 | tf_op jit(solution)/shard_map/ppermute | solution.py:228
  118.8 4.1 %collective-permute-start.6 = (bf16[256,1280]{1,0:T(8,128)(2,1)S(1)}, bf16[256,1280]{1,0:T(8,128)(2,1)S(1)}, u32[]{:S(2)}, u32[]{:S(2)}) collective-permute-start(bf16[256,1280]{1,0:T(8,128)(2,1)S(1)} %get-tuple-element.24), channel_id=1, source_target_pairs={{0,16},{16,0},{1,17},{17,1},{2,18},{18,2},{3,19},{19,3},{4,20},{20... | collective-permute-start | bytes 1966088 | tf_op jit(solution)/shard_map/ppermute | solution.py:228

commit v4 on v3

--- a/solution.py
+++ b/solution.py
@@ -13,7 +13,10 @@
 F32 = jnp.float32
 COEF = math.sqrt(2.0 / math.pi)
 PLANE = ("y", "x")
-COL = ("zh", "zl")
+TURN = 12
+RING = [(z + TURN) % 16 for z in range(16)]
+SHIFT = 4
+PARITIES = [[(TURN + p * (2 * SHIFT + 1) + 2 * q) % 16 for q in range(8)] for p in range(2)]
 SWAP = [(0, 1), (1, 0)]
 EVEN = [(z, z ^ 1) for z in range(16)]
 ODD = [(z, (((z - 1) ^ 1) + 1) % 16) for z in range(16)]
@@ -104,7 +107,8 @@
     part = 16
     parity = 1 - zl_ref[0] if flip else zl_ref[0]
     for q in range(rows.shape[0] // part):
-        begin = pl.multiple_of((2 * q + parity) * part, part)
+        block_at = 2 * lax.rem(q + SHIFT * parity, 8) + parity
+        begin = pl.multiple_of(block_at * part, part)
         rows[q * part : (q + 1) * part, :] = block[pl.ds(begin, part), :]
     output[:, :width] = matmul(rows[:, :hid], down[...], 1, 0).astype(BF16)
     output[:, width:] = matmul(rows[:, :hid], down2[...], 1, 0).astype(BF16)
@@ -178,7 +182,7 @@
     rows, width = activations.shape
     hid = up.shape[1]
     core = lax.axis_index("core").astype(jnp.int32).reshape(1)
-    zl = lax.axis_index("zl").astype(jnp.int32).reshape(1)
+    zl = (lax.axis_index("col") % 2).astype(jnp.int32).reshape(1)
     part = rows // 2
     half = 16 * part
     members = 16
@@ -190,7 +194,7 @@
         jnp.concatenate([activations, cotangent], axis=1), "core", axis=0, tiled=True
     )
     (mine,) = call(pick_kernel, [shape(part, 4 * width)], 8 * work, core, zl, pair)
-    panel = lax.all_gather(mine, COL, axis=0, tiled=True)
+    panel = lax.all_gather(mine, "col", axis=0, tiled=True, axis_index_groups=[RING])
 
     (partial,) = call(
         first_kernel, [shape(half, 2 * hid)], work, panel, up, down, up2, down2
@@ -215,13 +219,15 @@
         )
 
     send_out, send_in = second(True)
-    came_out = lax.ppermute(send_out, COL, EVEN)
-    came_in = lax.ppermute(send_in, COL, ODD)
+    came_out = lax.ppermute(send_out, "col", EVEN)
+    came_in = lax.ppermute(send_in, "col", ODD)
     keep_out, keep_in = second(False)
     (added,) = call(
         pair_kernel, [shape(half // 2, 4 * width)], 0, keep_out, came_out, keep_in, came_in
     )
-    gathered = lax.all_to_all(added, "zh", 0, 0, tiled=True)
+    gathered = lax.all_to_all(
+        added, "col", 0, 0, tiled=True, axis_index_groups=PARITIES
+    )
 
     piece = (2 * hid + 2 * width) // PIECES
     pieces = call(stage_kernel, [shape(half, piece)] * PIECES, work // 4, added, own, panel)
@@ -238,12 +244,12 @@
 
 
 def solution(mesh):
-    fine = Mesh(mesh.devices.reshape(4, 4, 2, 8, 2), ("y", "x", "core", "zh", "zl"))
+    fine = Mesh(mesh.devices.reshape(4, 4, 2, 16), ("y", "x", "core", "col"))
     row = ("y", "x", "core")
     return jax.shard_map(
         per_device,
         mesh=fine,
-        in_specs=(P(COL, row), P(row, COL), P(COL, row), P(COL, row)),
-        out_specs=(P(COL, row), P(COL, row), P(row, COL), P(COL, row)),
+        in_specs=(P("col", row), P(row, "col"), P("col", row), P("col", row)),
+        out_specs=(P("col", row), P("col", row), P(row, "col"), P("col", row)),
         check_vma=False,
     )

time: 134 us -> 132 us (0.985)
  blocking collectives: 77.1 us -> 73.9 us
  starting transfers between devices: 40.5 us -> 42.1 us
    all_gather x1, blocking collectives: 6.93 us -> 3.72 us  [per_device(): both = lax.all_gather(summed, 'core', axis=0, tiled=True)]
    all_to_all x1, starting transfers between devices: 7.12 us -> 8.48 us  [per_device(): lax.all_to_all(added, 'col', 0, 0, tiled=True, axis_index_groups=PARITIES)]
where the time goes in v4:
time: 132 us
  blocking collectives  73.9 us (56%)
  starting transfers between devices  42.1 us (32%)
  Pallas kernels  10.3 us (8%)
  waiting for transfers between devices  4.07 us (3%)
    all_gather x1, blocking collectives, per_device(): lax.all_gather(mine, 'col', axis=0, tiled=True, axis_index_groups=[RING])  27.7 us
    all_to_all x1, blocking collectives, per_device(): got = lax.all_to_all(partial, PLANE, 0, 0, tiled=True)  22.4 us
    all_to_all x1, blocking collectives, per_device(): own = lax.all_to_all(spread, PLANE, 0, 0, tiled=True)  17.9 us
    ppermute x3, starting transfers between devices, per_device(): others = [lax.ppermute(piece, 'core', SWAP) for piece in pieces]  17 us
    pallas_call x10, Pallas kernels, call(): pl.pallas_call(kernel, out_shape=out_shape, in_specs=specs, out_specs=[VM...  10.3 us
    ppermute x1, starting transfers between devices, per_device(): up2 = lax.ppermute(up, 'core', SWAP)  8.79 us
    all_to_all x1, starting transfers between devices, per_device(): lax.all_to_all(added, 'col', 0, 0, tiled=True, axis_index_groups=PARITIES)  8.48 us
    ppermute x1, starting transfers between devices, per_device(): came_in = lax.ppermute(send_in, 'col', ODD)  4 us
  transfers between devices with their start and end apart: 8, of which 2 were waited for; matrix products, arithmetic and copies ran while one was open for 1% of the time, Pallas kernels for 4%

profile of v4, /device:TPU:1, one launch (start us, length us, event | category | flops | bytes accessed | tf_op | source)
XLA Modules:
  0.0 131.9 jit_solution(16039917879125136668)
XLA Ops:
  0.6 8.8 %collective-permute-start = (bf16[384,1536]{1,0:T(8,128)(2,1)}, bf16[384,1536]{1,0:T(8,128)(2,1)S(1)}, u32[]{:S(2)}, u32[]{:S(2)}) collective-permute-start(bf16[384,1536]{1,0:T(8,128)(2,1)} %up.5), channel_id=1, source_target_pairs={{0,16},{16,0},{1,17},{17,1},{2,18},{18,2},{3,19},{19,3},{4,20},{20... | collective-permute-start | bytes 3538952 | tf_op jit(solution)/shard_map/ppermute | solution.py:191
  9.4 1.9 %collective-permute-start.1 = (bf16[1536,384]{1,0:T(8,128)(2,1)}, bf16[1536,384]{1,0:T(8,128)(2,1)S(1)}, u32[]{:S(2)}, u32[]{:S(2)}) collective-permute-start(bf16[1536,384]{1,0:T(8,128)(2,1)} %down.5), channel_id=1, source_target_pairs={{0,16},{16,0},{1,17},{17,1},{2,18},{18,2},{3,19},{19,3},{4,20},{20... | collective-permute-start | bytes 3538952 | tf_op jit(solution)/shard_map/ppermute | solution.py:192
  11.4 0.8 pad_maximum_fusion
  12.1 2.1 %all_gather.9.pair = bf16[64,768]{1,0:T(8,128)(2,1)S(1)} all-gather(bf16[32,768]{1,0:T(8,128)(2,1)S(1)} %pad_maximum_fusion), channel_id=1, replica_groups=mesh['y'=4,'x'=4,'core'=2,'col'=16] {'core'}, dimensions={0}, use_global_device_ids=true | all-gather | bytes 147456 | tf_op jit(solution)/shard_map/all_gather | solution.py:193
  14.2 0.0 copy-start
  14.2 0.0 copy-start.1
  14.3 27.7 %all_gather.10.panel = bf16[256,1536]{1,0:T(8,128)(2,1)S(1)} all-gather(bf16[16,1536]{1,0:T(8,128)(2,1)S(1)} %shard_map.75), channel_id=1, replica_groups={{12,13,14,15,0,1,2,3,4,5,6,7,8,9,10,11},{28,29,30,31,16,17,18,19,20,21,..., dimensions={0}, use_global_device_ids=true | all-gather | bytes 835584 | tf_op jit(solution)/shard_map/all_gather | solution.py:197
  42.0 0.0 collective-permute-done.up2
  42.0 0.0 collective-permute-done.1.down2
  42.0 0.0 copy-done
  42.0 0.0 copy-done.1
  42.0 0.0 copy-start.2
  42.0 1.8 %shard_map.76 = bf16[256,3072]{1,0:T(8,128)(2,1)S(1)} custom-call(bf16[256,1536]{1,0:T(8,128)(2,1)S(1)} %all_gather.10.panel, bf16[384,1536]{1,0:T(8,128)(2,1)S(1)} %copy-done, bf16[1536,384]{1,0:T(8,128)(2,1)S(1)} %copy-done.1, bf16[384,1536]{1,0:T(8,128)(2,1)S(1)} %collective-permute-done.up2, bf16[1536,384]{1,0:T(8,128)(2,1)S(1)} %collective-permute-done.1.down2), custom_call_target="tpu_custom_call" | custom-call | flops 1207959552 | bytes 7077888 | tf_op jit(solution)/shard_map/pallas_call | solution.py:46
  43.8 0.0 copy-done.2
  43.8 22.4 %all_to_all.34 = bf16[16,16,3072]{2,1,0:T(8,128)(2,1)S(1)} all-to-all(bf16[16,16,3072]{2,1,0:T(8,128)(2,1)S(1)} %bitcast.12), channel_id=1, replica_groups=mesh['y'=4,'x'=4,'core'=2,'col'=16] {'y','x'}, dimensions={0} | all-to-all | bytes 3145728 | tf_op jit(solution)/shard_map/all_to_all | solution.py:203
  66.2 0.3 shard_map.77
  66.5 0.0 copy-start.3
  66.5 17.9 %all_to_all.35 = bf16[16,16,3072]{2,1,0:T(8,128)(2,1)S(1)} all-to-all(bf16[16,16,3072]{2,1,0:T(8,128)(2,1)S(1)} %bitcast.14), channel_id=1, replica_groups=mesh['y'=4,'x'=4,'core'=2,'col'=16] {'y','x'}, dimensions={0} | all-to-all | bytes 3145728 | tf_op jit(solution)/shard_map/all_to_all | solution.py:205
  84.5 0.0 copy-done.3
  84.5 1.2 shard_map.79
  85.7 1.9 %collective-permute-start.2 = (bf16[128,768]{1,0:T(8,128)(2,1)S(1)}, bf16[128,768]{1,0:T(8,128)(2,1)S(1)}, u32[]{:S(2)}, u32[]{:S(2)}) collective-permute-start(bf16[128,768]{1,0:T(8,128)(2,1)S(1)} %get-tuple-element.19), channel_id=1, source_target_pairs={{0,1},{1,0},{2,3},{3,2},{4,5},{5,4},{6,7},{7,6},{8,9},{9,8},{10,11... | collective-permute-start | bytes 589832 | tf_op jit(solution)/shard_map/ppermute | solution.py:222
  87.7 4.0 %collective-permute-start.3 = (bf16[128,768]{1,0:T(8,128)(2,1)S(1)}, bf16[128,768]{1,0:T(8,128)(2,1)S(1)}, u32[]{:S(2)}, u32[]{:S(2)}) collective-permute-start(bf16[128,768]{1,0:T(8,128)(2,1)S(1)} %get-tuple-element.21), channel_id=1, source_target_pairs={{0,15},{1,2},{2,1},{3,4},{4,3},{5,6},{6,5},{7,8},{8,7},{9,10},{10,... | collective-permute-start | bytes 589832 | tf_op jit(solution)/shard_map/ppermute | solution.py:223
  91.7 1.2 shard_map.78
  92.9 0.0 collective-permute-done.2.came_a
  92.9 2.4 %collective-permute-done.3.came_b = bf16[128,768]{1,0:T(8,128)(2,1)S(1)} collective-permute-done((bf16[128,768]{1,0:T(8,128)(2,1)S(1)}, bf16[128,768]{1,0:T(8,128)(2,1)S(1)}, u32[]{:S(2)}, u32[]{:S(2)}) %collective-permute-start.3) | collective-permute-done | bytes 196640 | tf_op jit(solution)/shard_map/ppermute | solution.py:223
  95.3 0.9 shard_map.80._
  96.1 8.5 %all-to-all-start.2 = ((bf16[8,16,1536]{2,1,0:T(8,128)(2,1)}), bf16[8,16,1536]{2,1,0:T(8,128)(2,1)S(1)}, u32[]{:S(2)}, u32[]{:S(2)}) async-start(bf16[8,16,1536]{2,1,0:T(8,128)(2,1)} %bitcast.6), calls=%async_computation.2 | async-start | bytes 786432 | tf_op jit(solution)/shard_map/all_to_all | solution.py:228
  104.6 1.2 shard_map.81
  105.8 12.6 %collective-permute-start.4 = (bf16[256,1280]{1,0:T(8,128)(2,1)S(1)}, bf16[256,1280]{1,0:T(8,128)(2,1)S(1)}, u32[]{:S(2)}, u32[]{:S(2)}) collective-permute-start(bf16[256,1280]{1,0:T(8,128)(2,1)S(1)} %get-tuple-element.22), channel_id=1, source_target_pairs={{0,16},{16,0},{1,17},{17,1},{2,18},{18,2},{3,19},{19,3},{4,20},{20... | collective-permute-start | bytes 1966088 | tf_op jit(solution)/shard_map/ppermute | solution.py:234
  118.4 1.9 %collective-permute-start.5 = (bf16[256,1280]{1,0:T(8,128)(2,1)S(1)}, bf16[256,1280]{1,0:T(8,128)(2,1)S(1)}, u32[]{:S(2)}, u32[]{:S(2)}) collective-permute-start(bf16[256,1280]{1,0:T(8,128)(2,1)S(1)} %get-tuple-element.23), channel_id=1, source_target_pairs={{0,16},{16,0},{1,17},{17,1},{2,18},{18,2},{3,19},{19,3},{4,20},{20... | collective-permute-start | bytes 1966088 | tf_op jit(solution)/shard_map/ppermute | solution.py:234
  120.3 2.4 %collective-permute-start.6 = (bf16[256,1280]{1,0:T(8,128)(2,1)S(1)}, bf16[256,1280]{1,0:T(8,128)(2,1)S(1)}, u32[]{:S(2)}, u32[]{:S(2)}) collective-permute-start(bf16[256,1280]{1,0:T(8,128)(2,1)S(1)} %get-tuple-element.24), channel_id=1, source_target_pairs={{0,16},{16,0},{1,17},{17,1},{2,18},{18,2},{3,19},{19,3},{4,20},{20... | collective-permute-start | bytes 1966088 | tf_op jit(solution)/shard_map/ppermute | solution.py:234
  122.8 0.0 collective-permute-done.4.refs_0_
  122.8 0.0 collective-permute-done.5.refs_1_
  122.8 1.7 %collective-permute-done.6.refs_2_ = bf16[256,1280]{1,0:T(8,128)(2,1)S(1)} collective-permute-done((bf16[256,1280]{1,0:T(8,128)(2,1)S(1)}, bf16[256,1280]{1,0:T(8,128)(2,1)S(1)}, u32[]{:S(2)}, u32[]{:S(2)}) %collective-permute-start.6) | collective-permute-done | bytes 655392 | tf_op jit(solution)/shard_map/ppermute | solution.py:234
  124.5 3.0 %shard_map.82 = (bf16[384,1536]{1,0:T(8,128)(2,1)}, bf16[1536,384]{1,0:T(8,128)(2,1)}) custom-call(bf16[256,1536]{1,0:T(8,128)(2,1)S(1)} %all_gather.10.panel, bf16[256,3072]{1,0:T(8,128)(2,1)S(1)} %bitcast.11, bf16[256,1280]{1,0:T(8,128)(2,1)S(1)} %collective-permute-done.4.refs_0_, bf16[256,1280]{1,0:T(8,128)(2,1)S(1)} %collective-permute-done.5.refs_1_, ...), custom_call_target="tpu_custom_call" | custom-call | flops 1207959552 | bytes 6684672 | tf_op jit(solution)/shard_map/pallas_call | solution.py:46
  127.5 0.0 all-to-all-done.2
  127.5 0.1 shard_map.83
  127.5 3.7 %all_gather.11.both = bf16[32,1536]{1,0:T(8,128)(2,1)S(1)} all-gather(bf16[16,1536]{1,0:T(8,128)(2,1)S(1)} %shard_map.83), channel_id=1, replica_groups=mesh['y'=4,'x'=4,'core'=2,'col'=16] {'core'}, dimensions={0}, use_global_device_ids=true | all-gather | bytes 147456 | tf_op jit(solution)/shard_map/all_gather | solution.py:241
  131.3 0.6 shard_map.84
  (1 shorter events, 0.0 us)
Async XLA Ops:
  0.6 41.4 %collective-permute-start = (bf16[384,1536]{1,0:T(8,128)(2,1)}, bf16[384,1536]{1,0:T(8,128)(2,1)S(1)}, u32[]{:S(2)}, u32[]{:S(2)}) collective-permute-start(bf16[384,1536]{1,0:T(8,128)(2,1)} %up.5), channel_id=1, source_target_pairs={{0,16},{16,0},{1,17},{17,1},{2,18},{18,2},{3,19},{19,3},{4,20},{20... | collective-permute-start | bytes 3538952 | tf_op jit(solution)/shard_map/ppermute | solution.py:191
  9.4 32.6 %collective-permute-start.1 = (bf16[1536,384]{1,0:T(8,128)(2,1)}, bf16[1536,384]{1,0:T(8,128)(2,1)S(1)}, u32[]{:S(2)}, u32[]{:S(2)}) collective-permute-start(bf16[1536,384]{1,0:T(8,128)(2,1)} %down.5), channel_id=1, source_target_pairs={{0,16},{16,0},{1,17},{17,1},{2,18},{18,2},{3,19},{19,3},{4,20},{20... | collective-permute-start | bytes 3538952 | tf_op jit(solution)/shard_map/ppermute | solution.py:192
  14.2 27.7 %copy-start = (bf16[384,1536]{1,0:T(8,128)(2,1)S(1)}, bf16[384,1536]{1,0:T(8,128)(2,1)}, u32[]{:S(2)}) copy-start(bf16[384,1536]{1,0:T(8,128)(2,1)} %up.5) | copy-start | bytes 3538948
  14.2 27.8 %copy-start.1 = (bf16[1536,384]{1,0:T(8,128)(2,1)S(1)}, bf16[1536,384]{1,0:T(8,128)(2,1)}, u32[]{:S(2)}) copy-start(bf16[1536,384]{1,0:T(8,128)(2,1)} %down.5) | copy-start | bytes 3538948
  42.0 1.8 %copy-start.2 = (bf16[1536,384]{1,0:T(8,128)(2,1)}, bf16[1536,384]{1,0:T(8,128)(2,1)S(1)}, u32[]{:S(2)}) copy-start(bf16[1536,384]{1,0:T(8,128)(2,1)S(1)} %collective-permute-done.1.down2) | copy-start | bytes 3538948
  66.5 18.0 %copy-start.3 = (bf16[1536,384]{1,0:T(8,128)(2,1)S(1)}, bf16[1536,384]{1,0:T(8,128)(2,1)}, u32[]{:S(2)}) copy-start(bf16[1536,384]{1,0:T(8,128)(2,1)} %copy-done.2) | copy-start | bytes 3538948
  85.7 7.2 %collective-permute-start.2 = (bf16[128,768]{1,0:T(8,128)(2,1)S(1)}, bf16[128,768]{1,0:T(8,128)(2,1)S(1)}, u32[]{:S(2)}, u32[]{:S(2)}) collective-permute-start(bf16[128,768]{1,0:T(8,128)(2,1)S(1)} %get-tuple-element.19), channel_id=1, source_target_pairs={{0,1},{1,0},{2,3},{3,2},{4,5},{5,4},{6,7},{7,6},{8,9},{9,8},{10,11... | collective-permute-start | bytes 589832 | tf_op jit(solution)/shard_map/ppermute | solution.py:222
  87.7 7.6 %collective-permute-start.3 = (bf16[128,768]{1,0:T(8,128)(2,1)S(1)}, bf16[128,768]{1,0:T(8,128)(2,1)S(1)}, u32[]{:S(2)}, u32[]{:S(2)}) collective-permute-start(bf16[128,768]{1,0:T(8,128)(2,1)S(1)} %get-tuple-element.21), channel_id=1, source_target_pairs={{0,15},{1,2},{2,1},{3,4},{4,3},{5,6},{6,5},{7,8},{8,7},{9,10},{10,... | collective-permute-start | bytes 589832 | tf_op jit(solution)/shard_map/ppermute | solution.py:223
  96.1 31.4 %all-to-all-start.2 = ((bf16[8,16,1536]{2,1,0:T(8,128)(2,1)}), bf16[8,16,1536]{2,1,0:T(8,128)(2,1)S(1)}, u32[]{:S(2)}, u32[]{:S(2)}) async-start(bf16[8,16,1536]{2,1,0:T(8,128)(2,1)} %bitcast.6), calls=%async_computation.2 | async-start | bytes 786432 | tf_op jit(solution)/shard_map/all_to_all | solution.py:228
  105.8 17.0 %collective-permute-start.4 = (bf16[256,1280]{1,0:T(8,128)(2,1)S(1)}, bf16[256,1280]{1,0:T(8,128)(2,1)S(1)}, u32[]{:S(2)}, u32[]{:S(2)}) collective-permute-start(bf16[256,1280]{1,0:T(8,128)(2,1)S(1)} %get-tuple-element.22), channel_id=1, source_target_pairs={{0,16},{16,0},{1,17},{17,1},{2,18},{18,2},{3,19},{19,3},{4,20},{20... | collective-permute-start | bytes 1966088 | tf_op jit(solution)/shard_map/ppermute | solution.py:234
  118.4 4.4 %collective-permute-start.5 = (bf16[256,1280]{1,0:T(8,128)(2,1)S(1)}, bf16[256,1280]{1,0:T(8,128)(2,1)S(1)}, u32[]{:S(2)}, u32[]{:S(2)}) collective-permute-start(bf16[256,1280]{1,0:T(8,128)(2,1)S(1)} %get-tuple-element.23), channel_id=1, source_target_pairs={{0,16},{16,0},{1,17},{17,1},{2,18},{18,2},{3,19},{19,3},{4,20},{20... | collective-permute-start | bytes 1966088 | tf_op jit(solution)/shard_map/ppermute | solution.py:234
  120.3 4.1 %collective-permute-start.6 = (bf16[256,1280]{1,0:T(8,128)(2,1)S(1)}, bf16[256,1280]{1,0:T(8,128)(2,1)S(1)}, u32[]{:S(2)}, u32[]{:S(2)}) collective-permute-start(bf16[256,1280]{1,0:T(8,128)(2,1)S(1)} %get-tuple-element.24), channel_id=1, source_target_pairs={{0,16},{16,0},{1,17},{17,1},{2,18},{18,2},{3,19},{19,3},{4,20},{20... | collective-permute-start | bytes 1966088 | tf_op jit(solution)/shard_map/ppermute | solution.py:234

commit v5 on v4

--- a/solution.py
+++ b/solution.py
@@ -12,7 +12,7 @@
 BF16 = jnp.bfloat16
 F32 = jnp.float32
 COEF = math.sqrt(2.0 / math.pi)
-PLANE = ("y", "x")
+CHIPS = [list(range(15, -1, -1))]
 TURN = 12
 RING = [(z + TURN) % 16 for z in range(16)]
 SHIFT = 4
@@ -21,7 +21,6 @@
 EVEN = [(z, z ^ 1) for z in range(16)]
 ODD = [(z, (((z - 1) ^ 1) + 1) % 16) for z in range(16)]
 TILE = 256
-PIECES = 3
 MIB = 1024 * 1024
 VMEM = pl.BlockSpec(memory_space=pltpu.VMEM)
 SMEM = pl.BlockSpec(memory_space=pltpu.SMEM)
@@ -122,19 +121,13 @@
     out[:, cols:] = (keep_b[...].astype(F32) + came_b[...].astype(F32)).astype(BF16)
 
 
-def stage_kernel(_, own, panel, *outs):
-    cols = outs[0].shape[1]
-    split = own.shape[1]
-    for q, out in enumerate(outs):
-        begin, end = q * cols, (q + 1) * cols
-        if end <= split:
-            out[...] = own[:, begin:end]
-        else:
-            rest = panel.shape[1] // 2 + begin - split
-            if begin < split:
-                out[:, : split - begin] = own[:, begin:]
-                rest = panel.shape[1] // 2
-            out[:, max(split - begin, 0) :] = panel[:, rest : rest + end - max(split, begin)]
+def stage_kernel(_, own, panel, first, second):
+    hid = own.shape[1] // 2
+    width = panel.shape[1] // 4
+    first[:, :hid] = own[:, :hid]
+    first[:, hid:] = panel[:, 3 * width :]
+    second[:, :hid] = own[:, hid:]
+    second[:, hid:] = panel[:, 2 * width : 3 * width]
 
 
 def sum_kernel(parts, out):
@@ -158,23 +151,18 @@
         )
 
 
-def grads_kernel(panel, own, *refs):
-    *others, grad_up, grad_down = refs
+def grads_kernel(panel, own, first, second, grad_up, grad_down):
     width, hid = grad_up.shape
-    piece = others[0].shape[1]
-
-    def other(begin, size):
-        return others[begin // piece][:, begin % piece : begin % piece + size]
-
     act, cot = panel[:, :width], panel[:, width : 2 * width]
-    act2, cot2 = other(2 * hid, width), other(2 * hid + width, width)
+    act2, cot2 = second[:, hid:], first[:, hid:]
     for j in range(0, hid, TILE):
-        grad_down[j : j + TILE, :] = (
-            matmul(own[:, j : j + TILE], cot, 0, 0) + matmul(other(j, TILE), cot2, 0, 0)
-        ).astype(BF16)
-        grad_up[:, j : j + TILE] = (
+        cols = slice(j, j + TILE)
+        grad_down[cols, :] = (
+            matmul(own[:, cols], cot, 0, 0) + matmul(first[:, cols], cot2, 0, 0)
+        ).astype(BF16)
+        grad_up[:, cols] = (
             matmul(act, own[:, hid + j : hid + j + TILE], 0, 0)
-            + matmul(act2, other(hid + j, TILE), 0, 0)
+            + matmul(act2, second[:, cols], 0, 0)
         ).astype(BF16)
 
 
@@ -200,9 +188,9 @@
         first_kernel, [shape(half, 2 * hid)], work, panel, up, down, up2, down2
     )
 
-    got = lax.all_to_all(partial, PLANE, 0, 0, tiled=True)
+    got = lax.all_to_all(partial, "plane", 0, 0, tiled=True, axis_index_groups=CHIPS)
     (spread,) = call(middle_kernel, [shape(half, 2 * hid)], 8 * work, got)
-    own = lax.all_to_all(spread, PLANE, 0, 0, tiled=True)
+    own = lax.all_to_all(spread, "plane", 0, 0, tiled=True, axis_index_groups=CHIPS)
 
     def second(flip):
         return call(
@@ -229,8 +217,9 @@
         added, "col", 0, 0, tiled=True, axis_index_groups=PARITIES
     )
 
-    piece = (2 * hid + 2 * width) // PIECES
-    pieces = call(stage_kernel, [shape(half, piece)] * PIECES, work // 4, added, own, panel)
+    pieces = call(
+        stage_kernel, [shape(half, hid + width)] * 2, work // 4, added, own, panel
+    )
     others = [lax.ppermute(piece, "core", SWAP) for piece in pieces]
     grad_up, grad_down = call(
         grads_kernel, [shape(width, hid), shape(hid, width)], work, panel, own, *others
@@ -244,8 +233,8 @@
 
 
 def solution(mesh):
-    fine = Mesh(mesh.devices.reshape(4, 4, 2, 16), ("y", "x", "core", "col"))
-    row = ("y", "x", "core")
+    fine = Mesh(mesh.devices.reshape(16, 2, 16), ("plane", "core", "col"))
+    row = ("plane", "core")
     return jax.shard_map(
         per_device,
         mesh=fine,

time: 132 us -> 130 us (0.985)
  starting transfers between devices: 42.1 us -> 40 us
    all_to_all x2, blocking collectives: 40.3 us -> 37.6 us  [the longest x1 19.6 us: per_device(): lax.all_to_all(partial, 'plane', 0, 0, tiled=True, axis_index_groups=CHIPS)]
    ppermute x3 -> x2, starting transfers between devices: 17 us -> 14.8 us  [per_device(): others = [lax.ppermute(piece, 'core', SWAP) for piece in pieces]]
    all_gather x1, blocking collectives: 3.72 us -> 5.23 us  [per_device(): both = lax.all_gather(summed, 'core', axis=0, tiled=True)]
  transfers between devices with their start and end apart: 8 -> 7, of which waited for: 2 -> 3; matrix products, arithmetic and copies ran while one was open for 1% -> 1% of each run, Pallas kernels for 4% -> 4%
where the time goes in v5:
time: 130 us; the launch traced here: 129 us
  blocking collectives  72.6 us (56%)
  starting transfers between devices  40 us (31%)
  Pallas kernels  10.3 us (8%)
  waiting for transfers between devices  4.93 us (4%)
    all_gather x1, blocking collectives, per_device(): lax.all_gather(mine, 'col', axis=0, tiled=True, axis_index_groups=[RING])  27.7 us
    all_to_all x1, blocking collectives, per_device(): lax.all_to_all(partial, 'plane', 0, 0, tiled=True, axis_index_groups=CHIPS)  19.6 us
    all_to_all x1, blocking collectives, per_device(): lax.all_to_all(spread, 'plane', 0, 0, tiled=True, axis_index_groups=CHIPS)  18 us
    ppermute x2, starting transfers between devices, per_device(): others = [lax.ppermute(piece, 'core', SWAP) for piece in pieces]  14.8 us
    pallas_call x10, Pallas kernels, call(): pl.pallas_call(kernel, out_shape=out_shape, in_specs=specs, out_specs=[VM...  10.3 us
    ppermute x1, starting transfers between devices, per_device(): up2 = lax.ppermute(up, 'core', SWAP)  8.79 us
    all_to_all x1, starting transfers between devices, per_device(): lax.all_to_all(added, 'col', 0, 0, tiled=True, axis_index_groups=PARITIES)  8.51 us
    all_gather x1, blocking collectives, per_device(): both = lax.all_gather(summed, 'core', axis=0, tiled=True)  5.23 us
  transfers between devices with their start and end apart: 7, of which 3 were waited for; matrix products, arithmetic and copies ran while one was open for 1% of the time, Pallas kernels for 4%

profile of v5, /device:TPU:1, one launch (start us, length us, event | category | flops | bytes accessed | tf_op | source)
XLA Modules:
  0.0 129.4 jit_solution(5568118985245710481)
XLA Ops:
  0.6 8.8 %collective-permute-start = (bf16[384,1536]{1,0:T(8,128)(2,1)}, bf16[384,1536]{1,0:T(8,128)(2,1)S(1)}, u32[]{:S(2)}, u32[]{:S(2)}) collective-permute-start(bf16[384,1536]{1,0:T(8,128)(2,1)} %up.5), channel_id=1, source_target_pairs={{0,16},{16,0},{1,17},{17,1},{2,18},{18,2},{3,19},{19,3},{4,20},{20... | collective-permute-start | bytes 3538952 | tf_op jit(solution)/shard_map/ppermute | solution.py:179
  9.4 1.9 %collective-permute-start.1 = (bf16[1536,384]{1,0:T(8,128)(2,1)}, bf16[1536,384]{1,0:T(8,128)(2,1)S(1)}, u32[]{:S(2)}, u32[]{:S(2)}) collective-permute-start(bf16[1536,384]{1,0:T(8,128)(2,1)} %down.5), channel_id=1, source_target_pairs={{0,16},{16,0},{1,17},{17,1},{2,18},{18,2},{3,19},{19,3},{4,20},{20... | collective-permute-start | bytes 3538952 | tf_op jit(solution)/shard_map/ppermute | solution.py:180
  11.4 0.8 pad_maximum_fusion
  12.1 2.1 %all_gather.9.pair = bf16[64,768]{1,0:T(8,128)(2,1)S(1)} all-gather(bf16[32,768]{1,0:T(8,128)(2,1)S(1)} %pad_maximum_fusion), channel_id=1, replica_groups=mesh['plane'=16,'core'=2,'col'=16] {'core'}, dimensions={0}, use_global_device_ids=true | all-gather | bytes 147456 | tf_op jit(solution)/shard_map/all_gather | solution.py:181
  14.2 0.0 copy-start
  14.2 0.0 copy-start.1
  14.3 27.7 %all_gather.10.panel = bf16[256,1536]{1,0:T(8,128)(2,1)S(1)} all-gather(bf16[16,1536]{1,0:T(8,128)(2,1)S(1)} %shard_map.75), channel_id=1, replica_groups={{12,13,14,15,0,1,2,3,4,5,6,7,8,9,10,11},{28,29,30,31,16,17,18,19,20,21,..., dimensions={0}, use_global_device_ids=true | all-gather | bytes 835584 | tf_op jit(solution)/shard_map/all_gather | solution.py:185
  42.0 0.0 collective-permute-done.up2
  42.0 0.0 collective-permute-done.1.down2
  42.0 0.0 copy-done
  42.0 0.0 copy-done.1
  42.0 0.0 copy-start.2
  42.0 1.8 %shard_map.76 = bf16[256,3072]{1,0:T(8,128)(2,1)S(1)} custom-call(bf16[256,1536]{1,0:T(8,128)(2,1)S(1)} %all_gather.10.panel, bf16[384,1536]{1,0:T(8,128)(2,1)S(1)} %copy-done, bf16[1536,384]{1,0:T(8,128)(2,1)S(1)} %copy-done.1, bf16[384,1536]{1,0:T(8,128)(2,1)S(1)} %collective-permute-done.up2, bf16[1536,384]{1,0:T(8,128)(2,1)S(1)} %collective-permute-done.1.down2), custom_call_target="tpu_custom_call" | custom-call | flops 1207959552 | bytes 7077888 | tf_op jit(solution)/shard_map/pallas_call | solution.py:45
  43.8 0.0 copy-done.2
  43.8 19.6 %all_to_all.34 = bf16[16,16,3072]{2,1,0:T(8,128)(2,1)S(1)} all-to-all(bf16[16,16,3072]{2,1,0:T(8,128)(2,1)S(1)} %bitcast.12), channel_id=1, replica_groups={{480,448,416,384,352,320,288,256,224,192,160,128,96,64,32,0},{481,449,4..., dimensions={0} | all-to-all | bytes 3145728 | tf_op jit(solution)/shard_map/all_to_all | solution.py:191
  63.4 0.3 shard_map.77
  63.7 0.0 copy-start.3
  63.8 18.0 %all_to_all.35 = bf16[16,16,3072]{2,1,0:T(8,128)(2,1)S(1)} all-to-all(bf16[16,16,3072]{2,1,0:T(8,128)(2,1)S(1)} %bitcast.14), channel_id=1, replica_groups={{480,448,416,384,352,320,288,256,224,192,160,128,96,64,32,0},{481,449,4..., dimensions={0} | all-to-all | bytes 3145728 | tf_op jit(solution)/shard_map/all_to_all | solution.py:193
  81.7 0.0 copy-done.3
  81.7 1.2 shard_map.79
  83.0 1.9 %collective-permute-start.2 = (bf16[128,768]{1,0:T(8,128)(2,1)S(1)}, bf16[128,768]{1,0:T(8,128)(2,1)S(1)}, u32[]{:S(2)}, u32[]{:S(2)}) collective-permute-start(bf16[128,768]{1,0:T(8,128)(2,1)S(1)} %get-tuple-element.18), channel_id=1, source_target_pairs={{0,1},{1,0},{2,3},{3,2},{4,5},{5,4},{6,7},{7,6},{8,9},{9,8},{10,11... | collective-permute-start | bytes 589832 | tf_op jit(solution)/shard_map/ppermute | solution.py:210
  84.9 4.0 %collective-permute-start.3 = (bf16[128,768]{1,0:T(8,128)(2,1)S(1)}, bf16[128,768]{1,0:T(8,128)(2,1)S(1)}, u32[]{:S(2)}, u32[]{:S(2)}) collective-permute-start(bf16[128,768]{1,0:T(8,128)(2,1)S(1)} %get-tuple-element.20), channel_id=1, source_target_pairs={{0,15},{1,2},{2,1},{3,4},{4,3},{5,6},{6,5},{7,8},{8,7},{9,10},{10,... | collective-permute-start | bytes 589832 | tf_op jit(solution)/shard_map/ppermute | solution.py:211
  88.9 1.2 shard_map.78
  90.1 0.0 collective-permute-done.2.came_a
  90.1 2.4 %collective-permute-done.3.came_b = bf16[128,768]{1,0:T(8,128)(2,1)S(1)} collective-permute-done((bf16[128,768]{1,0:T(8,128)(2,1)S(1)}, bf16[128,768]{1,0:T(8,128)(2,1)S(1)}, u32[]{:S(2)}, u32[]{:S(2)}) %collective-permute-start.3) | collective-permute-done | bytes 196640 | tf_op jit(solution)/shard_map/ppermute | solution.py:211
  92.5 0.9 shard_map.80._
  93.4 8.5 %all-to-all-start.2 = ((bf16[8,16,1536]{2,1,0:T(8,128)(2,1)}), bf16[8,16,1536]{2,1,0:T(8,128)(2,1)S(1)}, u32[]{:S(2)}, u32[]{:S(2)}) async-start(bf16[8,16,1536]{2,1,0:T(8,128)(2,1)} %bitcast.6), calls=%async_computation.2 | async-start | bytes 786432 | tf_op jit(solution)/shard_map/all_to_all | solution.py:216
  101.9 1.2 shard_map.81
  103.1 12.9 %collective-permute-start.4 = (bf16[256,1920]{1,0:T(8,128)(2,1)S(1)}, bf16[256,1920]{1,0:T(8,128)(2,1)S(1)}, u32[]{:S(2)}, u32[]{:S(2)}) collective-permute-start(bf16[256,1920]{1,0:T(8,128)(2,1)S(1)} %get-tuple-element.21), channel_id=1, source_target_pairs={{0,16},{16,0},{1,17},{17,1},{2,18},{18,2},{3,19},{19,3},{4,20},{20... | collective-permute-start | bytes 2949128 | tf_op jit(solution)/shard_map/ppermute | solution.py:223
  116.0 1.9 %collective-permute-start.5 = (bf16[256,1920]{1,0:T(8,128)(2,1)S(1)}, bf16[256,1920]{1,0:T(8,128)(2,1)S(1)}, u32[]{:S(2)}, u32[]{:S(2)}) collective-permute-start(bf16[256,1920]{1,0:T(8,128)(2,1)S(1)} %get-tuple-element.22), channel_id=1, source_target_pairs={{0,16},{16,0},{1,17},{17,1},{2,18},{18,2},{3,19},{19,3},{4,20},{20... | collective-permute-start | bytes 2949128 | tf_op jit(solution)/shard_map/ppermute | solution.py:223
  117.9 0.2 collective-permute-done.4.first
  118.2 2.3 %collective-permute-done.5.second = bf16[256,1920]{1,0:T(8,128)(2,1)S(1)} collective-permute-done((bf16[256,1920]{1,0:T(8,128)(2,1)S(1)}, bf16[256,1920]{1,0:T(8,128)(2,1)S(1)}, u32[]{:S(2)}, u32[]{:S(2)}) %collective-permute-start.5) | collective-permute-done | bytes 983072 | tf_op jit(solution)/shard_map/ppermute | solution.py:223
  120.4 3.0 %shard_map.82 = (bf16[384,1536]{1,0:T(8,128)(2,1)}, bf16[1536,384]{1,0:T(8,128)(2,1)}) custom-call(bf16[256,1536]{1,0:T(8,128)(2,1)S(1)} %all_gather.10.panel, bf16[256,3072]{1,0:T(8,128)(2,1)S(1)} %bitcast.11, bf16[256,1920]{1,0:T(8,128)(2,1)S(1)} %collective-permute-done.4.first, bf16[256,1920]{1,0:T(8,128)(2,1)S(1)} %collective-permute-done.5.second), custom_call_target="tpu_custom_call" | custom-call | flops 1207959552 | bytes 6684672 | tf_op jit(solution)/shard_map/pallas_call | solution.py:45
  123.5 0.0 all-to-all-done.2
  123.5 0.1 shard_map.83
  123.5 5.2 %all_gather.11.both = bf16[32,1536]{1,0:T(8,128)(2,1)S(1)} all-gather(bf16[16,1536]{1,0:T(8,128)(2,1)S(1)} %shard_map.83), channel_id=1, replica_groups=mesh['plane'=16,'core'=2,'col'=16] {'core'}, dimensions={0}, use_global_device_ids=true | all-gather | bytes 147456 | tf_op jit(solution)/shard_map/all_gather | solution.py:230
  128.8 0.6 shard_map.84
  (1 shorter events, 0.0 us)
Async XLA Ops:
  0.6 41.4 %collective-permute-start = (bf16[384,1536]{1,0:T(8,128)(2,1)}, bf16[384,1536]{1,0:T(8,128)(2,1)S(1)}, u32[]{:S(2)}, u32[]{:S(2)}) collective-permute-start(bf16[384,1536]{1,0:T(8,128)(2,1)} %up.5), channel_id=1, source_target_pairs={{0,16},{16,0},{1,17},{17,1},{2,18},{18,2},{3,19},{19,3},{4,20},{20... | collective-permute-start | bytes 3538952 | tf_op jit(solution)/shard_map/ppermute | solution.py:179
  9.4 32.6 %collective-permute-start.1 = (bf16[1536,384]{1,0:T(8,128)(2,1)}, bf16[1536,384]{1,0:T(8,128)(2,1)S(1)}, u32[]{:S(2)}, u32[]{:S(2)}) collective-permute-start(bf16[1536,384]{1,0:T(8,128)(2,1)} %down.5), channel_id=1, source_target_pairs={{0,16},{16,0},{1,17},{17,1},{2,18},{18,2},{3,19},{19,3},{4,20},{20... | collective-permute-start | bytes 3538952 | tf_op jit(solution)/shard_map/ppermute | solution.py:180
  14.2 27.7 %copy-start = (bf16[384,1536]{1,0:T(8,128)(2,1)S(1)}, bf16[384,1536]{1,0:T(8,128)(2,1)}, u32[]{:S(2)}) copy-start(bf16[384,1536]{1,0:T(8,128)(2,1)} %up.5) | copy-start | bytes 3538948
  14.2 27.8 %copy-start.1 = (bf16[1536,384]{1,0:T(8,128)(2,1)S(1)}, bf16[1536,384]{1,0:T(8,128)(2,1)}, u32[]{:S(2)}) copy-start(bf16[1536,384]{1,0:T(8,128)(2,1)} %down.5) | copy-start | bytes 3538948
  42.0 1.8 %copy-start.2 = (bf16[1536,384]{1,0:T(8,128)(2,1)}, bf16[1536,384]{1,0:T(8,128)(2,1)S(1)}, u32[]{:S(2)}) copy-start(bf16[1536,384]{1,0:T(8,128)(2,1)S(1)} %collective-permute-done.1.down2) | copy-start | bytes 3538948
  63.7 18.0 %copy-start.3 = (bf16[1536,384]{1,0:T(8,128)(2,1)S(1)}, bf16[1536,384]{1,0:T(8,128)(2,1)}, u32[]{:S(2)}) copy-start(bf16[1536,384]{1,0:T(8,128)(2,1)} %copy-done.2) | copy-start | bytes 3538948
  83.0 7.2 %collective-permute-start.2 = (bf16[128,768]{1,0:T(8,128)(2,1)S(1)}, bf16[128,768]{1,0:T(8,128)(2,1)S(1)}, u32[]{:S(2)}, u32[]{:S(2)}) collective-permute-start(bf16[128,768]{1,0:T(8,128)(2,1)S(1)} %get-tuple-element.18), channel_id=1, source_target_pairs={{0,1},{1,0},{2,3},{3,2},{4,5},{5,4},{6,7},{7,6},{8,9},{9,8},{10,11... | collective-permute-start | bytes 589832 | tf_op jit(solution)/shard_map/ppermute | solution.py:210
  84.9 7.6 %collective-permute-start.3 = (bf16[128,768]{1,0:T(8,128)(2,1)S(1)}, bf16[128,768]{1,0:T(8,128)(2,1)S(1)}, u32[]{:S(2)}, u32[]{:S(2)}) collective-permute-start(bf16[128,768]{1,0:T(8,128)(2,1)S(1)} %get-tuple-element.20), channel_id=1, source_target_pairs={{0,15},{1,2},{2,1},{3,4},{4,3},{5,6},{6,5},{7,8},{8,7},{9,10},{10,... | collective-permute-start | bytes 589832 | tf_op jit(solution)/shard_map/ppermute | solution.py:211
  93.4 30.1 %all-to-all-start.2 = ((bf16[8,16,1536]{2,1,0:T(8,128)(2,1)}), bf16[8,16,1536]{2,1,0:T(8,128)(2,1)S(1)}, u32[]{:S(2)}, u32[]{:S(2)}) async-start(bf16[8,16,1536]{2,1,0:T(8,128)(2,1)} %bitcast.6), calls=%async_computation.2 | async-start | bytes 786432 | tf_op jit(solution)/shard_map/all_to_all | solution.py:216
  103.1 15.1 %collective-permute-start.4 = (bf16[256,1920]{1,0:T(8,128)(2,1)S(1)}, bf16[256,1920]{1,0:T(8,128)(2,1)S(1)}, u32[]{:S(2)}, u32[]{:S(2)}) collective-permute-start(bf16[256,1920]{1,0:T(8,128)(2,1)S(1)} %get-tuple-element.21), channel_id=1, source_target_pairs={{0,16},{16,0},{1,17},{17,1},{2,18},{18,2},{3,19},{19,3},{4,20},{20... | collective-permute-start | bytes 2949128 | tf_op jit(solution)/shard_map/ppermute | solution.py:223
  116.0 4.5 %collective-permute-start.5 = (bf16[256,1920]{1,0:T(8,128)(2,1)S(1)}, bf16[256,1920]{1,0:T(8,128)(2,1)S(1)}, u32[]{:S(2)}, u32[]{:S(2)}) collective-permute-start(bf16[256,1920]{1,0:T(8,128)(2,1)S(1)} %get-tuple-element.22), channel_id=1, source_target_pairs={{0,16},{16,0},{1,17},{17,1},{2,18},{18,2},{3,19},{19,3},{4,20},{20... | collective-permute-start | bytes 2949128 | tf_op jit(solution)/shard_map/ppermute | solution.py:223

commit v6 on v5

--- a/solution.py
+++ b/solution.py
@@ -19,7 +19,6 @@
 PARITIES = [[(TURN + p * (2 * SHIFT + 1) + 2 * q) % 16 for q in range(8)] for p in range(2)]
 SWAP = [(0, 1), (1, 0)]
 EVEN = [(z, z ^ 1) for z in range(16)]
-ODD = [(z, (((z - 1) ^ 1) + 1) % 16) for z in range(16)]
 TILE = 256
 MIB = 1024 * 1024
 VMEM = pl.BlockSpec(memory_space=pltpu.VMEM)
@@ -101,7 +100,7 @@
             spread[q * part : (q + 1) * part, there] = slope
 
 
-def second_kernel(flip, zl_ref, block, up, down, up2, down2, output, grad_input, rows):
+def second_kernel(flip, zl_ref, block, up, down, up2, down2, out, rows):
     width, hid = up.shape
     part = 16
     parity = 1 - zl_ref[0] if flip else zl_ref[0]
@@ -109,16 +108,14 @@
         block_at = 2 * lax.rem(q + SHIFT * parity, 8) + parity
         begin = pl.multiple_of(block_at * part, part)
         rows[q * part : (q + 1) * part, :] = block[pl.ds(begin, part), :]
-    output[:, :width] = matmul(rows[:, :hid], down[...], 1, 0).astype(BF16)
-    output[:, width:] = matmul(rows[:, :hid], down2[...], 1, 0).astype(BF16)
-    grad_input[:, :width] = matmul(rows[:, hid:], up[...], 1, 1).astype(BF16)
-    grad_input[:, width:] = matmul(rows[:, hid:], up2[...], 1, 1).astype(BF16)
-
-
-def pair_kernel(keep_a, came_a, keep_b, came_b, out):
-    cols = keep_a.shape[1]
-    out[:, :cols] = (keep_a[...].astype(F32) + came_a[...].astype(F32)).astype(BF16)
-    out[:, cols:] = (keep_b[...].astype(F32) + came_b[...].astype(F32)).astype(BF16)
+    out[:, :width] = matmul(rows[:, :hid], down[...], 1, 0).astype(BF16)
+    out[:, width : 2 * width] = matmul(rows[:, :hid], down2[...], 1, 0).astype(BF16)
+    out[:, 2 * width : 3 * width] = matmul(rows[:, hid:], up[...], 1, 1).astype(BF16)
+    out[:, 3 * width :] = matmul(rows[:, hid:], up2[...], 1, 1).astype(BF16)
+
+
+def pair_kernel(keep, came, out):
+    out[...] = (keep[...].astype(F32) + came[...].astype(F32)).astype(BF16)
 
 
 def stage_kernel(_, own, panel, first, second):
@@ -195,7 +192,7 @@
     def second(flip):
         return call(
             functools.partial(second_kernel, flip),
-            [shape(half // 2, 2 * width)] * 2,
+            [shape(half // 2, 4 * width)],
             work // 2,
             zl,
             own,
@@ -206,13 +203,10 @@
             scratch=[pltpu.VMEM((half // 2, 2 * hid), BF16)],
         )
 
-    send_out, send_in = second(True)
-    came_out = lax.ppermute(send_out, "col", EVEN)
-    came_in = lax.ppermute(send_in, "col", ODD)
-    keep_out, keep_in = second(False)
-    (added,) = call(
-        pair_kernel, [shape(half // 2, 4 * width)], 0, keep_out, came_out, keep_in, came_in
-    )
+    (send,) = second(True)
+    came = lax.ppermute(send, "col", EVEN)
+    (keep,) = second(False)
+    (added,) = call(pair_kernel, [shape(half // 2, 4 * width)], 0, keep, came)
     gathered = lax.all_to_all(
         added, "col", 0, 0, tiled=True, axis_index_groups=PARITIES
     )

time: 130 us -> 129 us (level)
  starting transfers between devices: 40 us -> 35.9 us
  waiting for transfers between devices: 4.93 us -> 7.89 us
    ppermute x2 -> x1, starting transfers between devices: 5.9 us -> 1.92 us  [per_device(): came = lax.ppermute(send, 'col', EVEN)]
    ppermute x2 -> x1, waiting for transfers between devices: 2.39 us -> 5.35 us  [per_device(): came = lax.ppermute(send, 'col', EVEN)]
  transfers between devices with their start and end apart: 7 -> 6, of which waited for: 3 -> 3; matrix products, arithmetic and copies ran while one was open for 1% -> 1% of each run, Pallas kernels for 4% -> 4%
where the time goes in v6:
time: 129 us; the launch traced here: 128 us
  blocking collectives  72.4 us (56%)
  starting transfers between devices  35.9 us (28%)
  Pallas kernels  10.3 us (8%)
  waiting for transfers between devices  7.89 us (6%)
    all_gather x1, blocking collectives, per_device(): lax.all_gather(mine, 'col', axis=0, tiled=True, axis_index_groups=[RING])  27.7 us
    all_to_all x1, blocking collectives, per_device(): lax.all_to_all(partial, 'plane', 0, 0, tiled=True, axis_index_groups=CHIPS)  19.6 us
    all_to_all x1, blocking collectives, per_device(): lax.all_to_all(spread, 'plane', 0, 0, tiled=True, axis_index_groups=CHIPS)  18 us
    ppermute x2, starting transfers between devices, per_device(): others = [lax.ppermute(piece, 'core', SWAP) for piece in pieces]  15 us
    pallas_call x10, Pallas kernels, call(): pl.pallas_call(kernel, out_shape=out_shape, in_specs=specs, out_specs=[VM...  10.3 us
    ppermute x1, starting transfers between devices, per_device(): up2 = lax.ppermute(up, 'core', SWAP)  8.79 us
    all_to_all x1, starting transfers between devices, per_device(): lax.all_to_all(added, 'col', 0, 0, tiled=True, axis_index_groups=PARITIES)  8.27 us
    ppermute x1, waiting for transfers between devices, per_device(): came = lax.ppermute(send, 'col', EVEN)  5.35 us
  transfers between devices with their start and end apart: 6, of which 3 were waited for; matrix products, arithmetic and copies ran while one was open for 1% of the time, Pallas kernels for 4%

profile of v6, /device:TPU:1, one launch (start us, length us, event | category | flops | bytes accessed | tf_op | source)
XLA Modules:
  0.0 128.0 jit_solution(5669604351601708845)
XLA Ops:
  0.6 8.8 %collective-permute-start = (bf16[384,1536]{1,0:T(8,128)(2,1)}, bf16[384,1536]{1,0:T(8,128)(2,1)S(1)}, u32[]{:S(2)}, u32[]{:S(2)}) collective-permute-start(bf16[384,1536]{1,0:T(8,128)(2,1)} %up.5), channel_id=1, source_target_pairs={{0,16},{16,0},{1,17},{17,1},{2,18},{18,2},{3,19},{19,3},{4,20},{20... | collective-permute-start | bytes 3538952 | tf_op jit(solution)/shard_map/ppermute | solution.py:176
  9.4 1.9 %collective-permute-start.1 = (bf16[1536,384]{1,0:T(8,128)(2,1)}, bf16[1536,384]{1,0:T(8,128)(2,1)S(1)}, u32[]{:S(2)}, u32[]{:S(2)}) collective-permute-start(bf16[1536,384]{1,0:T(8,128)(2,1)} %down.5), channel_id=1, source_target_pairs={{0,16},{16,0},{1,17},{17,1},{2,18},{18,2},{3,19},{19,3},{4,20},{20... | collective-permute-start | bytes 3538952 | tf_op jit(solution)/shard_map/ppermute | solution.py:177
  11.4 0.8 pad_maximum_fusion
  12.1 2.1 %all_gather.9.pair = bf16[64,768]{1,0:T(8,128)(2,1)S(1)} all-gather(bf16[32,768]{1,0:T(8,128)(2,1)S(1)} %pad_maximum_fusion), channel_id=1, replica_groups=mesh['plane'=16,'core'=2,'col'=16] {'core'}, dimensions={0}, use_global_device_ids=true | all-gather | bytes 147456 | tf_op jit(solution)/shard_map/all_gather | solution.py:178
  14.2 0.0 copy-start
  14.2 0.0 copy-start.1
  14.3 27.7 %all_gather.10.panel = bf16[256,1536]{1,0:T(8,128)(2,1)S(1)} all-gather(bf16[16,1536]{1,0:T(8,128)(2,1)S(1)} %shard_map.75), channel_id=1, replica_groups={{12,13,14,15,0,1,2,3,4,5,6,7,8,9,10,11},{28,29,30,31,16,17,18,19,20,21,..., dimensions={0}, use_global_device_ids=true | all-gather | bytes 835584 | tf_op jit(solution)/shard_map/all_gather | solution.py:182
  42.0 0.0 collective-permute-done.up2
  42.0 0.0 collective-permute-done.1.down2
  42.0 0.0 copy-done
  42.0 0.0 copy-done.1
  42.0 0.0 copy-start.2
  42.0 1.8 %shard_map.76 = bf16[256,3072]{1,0:T(8,128)(2,1)S(1)} custom-call(bf16[256,1536]{1,0:T(8,128)(2,1)S(1)} %all_gather.10.panel, bf16[384,1536]{1,0:T(8,128)(2,1)S(1)} %copy-done, bf16[1536,384]{1,0:T(8,128)(2,1)S(1)} %copy-done.1, bf16[384,1536]{1,0:T(8,128)(2,1)S(1)} %collective-permute-done.up2, bf16[1536,384]{1,0:T(8,128)(2,1)S(1)} %collective-permute-done.1.down2), custom_call_target="tpu_custom_call" | custom-call | flops 1207959552 | bytes 7077888 | tf_op jit(solution)/shard_map/pallas_call | solution.py:44
  43.8 0.0 copy-done.2
  43.8 19.6 %all_to_all.34 = bf16[16,16,3072]{2,1,0:T(8,128)(2,1)S(1)} all-to-all(bf16[16,16,3072]{2,1,0:T(8,128)(2,1)S(1)} %bitcast.12), channel_id=1, replica_groups={{480,448,416,384,352,320,288,256,224,192,160,128,96,64,32,0},{481,449,4..., dimensions={0} | all-to-all | bytes 3145728 | tf_op jit(solution)/shard_map/all_to_all | solution.py:188
  63.4 0.3 shard_map.77
  63.7 0.0 copy-start.3
  63.8 18.0 %all_to_all.35 = bf16[16,16,3072]{2,1,0:T(8,128)(2,1)S(1)} all-to-all(bf16[16,16,3072]{2,1,0:T(8,128)(2,1)S(1)} %bitcast.14), channel_id=1, replica_groups={{480,448,416,384,352,320,288,256,224,192,160,128,96,64,32,0},{481,449,4..., dimensions={0} | all-to-all | bytes 3145728 | tf_op jit(solution)/shard_map/all_to_all | solution.py:190
  81.7 0.0 copy-done.3
  81.7 1.2 shard_map.79
  83.0 1.9 %collective-permute-start.2 = (bf16[128,1536]{1,0:T(8,128)(2,1)S(1)}, bf16[128,1536]{1,0:T(8,128)(2,1)S(1)}, u32[]{:S(2)}, u32[]{:S(2)}) collective-permute-start(bf16[128,1536]{1,0:T(8,128)(2,1)S(1)} %shard_map.79), channel_id=1, source_target_pairs={{0,1},{1,0},{2,3},{3,2},{4,5},{5,4},{6,7},{7,6},{8,9},{9,8},{10,11... | collective-permute-start | bytes 1179656 | tf_op jit(solution)/shard_map/ppermute | solution.py:207
  84.9 1.2 shard_map.78.keep
  86.1 5.4 %collective-permute-done.2.came = bf16[128,1536]{1,0:T(8,128)(2,1)S(1)} collective-permute-done((bf16[128,1536]{1,0:T(8,128)(2,1)S(1)}, bf16[128,1536]{1,0:T(8,128)(2,1)S(1)}, u32[]{:S(2)}, u32[]{:S(2)}) %collective-permute-start.2) | collective-permute-done | bytes 393248 | tf_op jit(solution)/shard_map/ppermute | solution.py:207
  91.5 0.8 shard_map.80._
  92.3 8.3 %all-to-all-start.2 = ((bf16[8,16,1536]{2,1,0:T(8,128)(2,1)}), bf16[8,16,1536]{2,1,0:T(8,128)(2,1)S(1)}, u32[]{:S(2)}, u32[]{:S(2)}) async-start(bf16[8,16,1536]{2,1,0:T(8,128)(2,1)} %bitcast.6), calls=%async_computation.2 | async-start | bytes 786432 | tf_op jit(solution)/shard_map/all_to_all | solution.py:210
  100.6 1.2 shard_map.81
  101.8 13.1 %collective-permute-start.3 = (bf16[256,1920]{1,0:T(8,128)(2,1)S(1)}, bf16[256,1920]{1,0:T(8,128)(2,1)S(1)}, u32[]{:S(2)}, u32[]{:S(2)}) collective-permute-start(bf16[256,1920]{1,0:T(8,128)(2,1)S(1)} %get-tuple-element.13), channel_id=1, source_target_pairs={{0,16},{16,0},{1,17},{17,1},{2,18},{18,2},{3,19},{19,3},{4,20},{20... | collective-permute-start | bytes 2949128 | tf_op jit(solution)/shard_map/ppermute | solution.py:217
  114.9 1.9 %collective-permute-start.4 = (bf16[256,1920]{1,0:T(8,128)(2,1)S(1)}, bf16[256,1920]{1,0:T(8,128)(2,1)S(1)}, u32[]{:S(2)}, u32[]{:S(2)}) collective-permute-start(bf16[256,1920]{1,0:T(8,128)(2,1)S(1)} %get-tuple-element.14), channel_id=1, source_target_pairs={{0,16},{16,0},{1,17},{17,1},{2,18},{18,2},{3,19},{19,3},{4,20},{20... | collective-permute-start | bytes 2949128 | tf_op jit(solution)/shard_map/ppermute | solution.py:217
  116.8 0.2 collective-permute-done.3.first
  117.1 2.3 %collective-permute-done.4.second = bf16[256,1920]{1,0:T(8,128)(2,1)S(1)} collective-permute-done((bf16[256,1920]{1,0:T(8,128)(2,1)S(1)}, bf16[256,1920]{1,0:T(8,128)(2,1)S(1)}, u32[]{:S(2)}, u32[]{:S(2)}) %collective-permute-start.4) | collective-permute-done | bytes 983072 | tf_op jit(solution)/shard_map/ppermute | solution.py:217
  119.3 3.0 %shard_map.82 = (bf16[384,1536]{1,0:T(8,128)(2,1)}, bf16[1536,384]{1,0:T(8,128)(2,1)}) custom-call(bf16[256,1536]{1,0:T(8,128)(2,1)S(1)} %all_gather.10.panel, bf16[256,3072]{1,0:T(8,128)(2,1)S(1)} %bitcast.11, bf16[256,1920]{1,0:T(8,128)(2,1)S(1)} %collective-permute-done.3.first, bf16[256,1920]{1,0:T(8,128)(2,1)S(1)} %collective-permute-done.4.second), custom_call_target="tpu_custom_call" | custom-call | flops 1207959552 | bytes 6684672 | tf_op jit(solution)/shard_map/pallas_call | solution.py:44
  122.4 0.0 all-to-all-done.2
  122.4 0.1 shard_map.83
  122.4 5.0 %all_gather.11.both = bf16[32,1536]{1,0:T(8,128)(2,1)S(1)} all-gather(bf16[16,1536]{1,0:T(8,128)(2,1)S(1)} %shard_map.83), channel_id=1, replica_groups=mesh['plane'=16,'core'=2,'col'=16] {'core'}, dimensions={0}, use_global_device_ids=true | all-gather | bytes 147456 | tf_op jit(solution)/shard_map/all_gather | solution.py:224
  127.4 0.6 shard_map.84
  (1 shorter events, 0.0 us)
Async XLA Ops:
  0.6 41.4 %collective-permute-start = (bf16[384,1536]{1,0:T(8,128)(2,1)}, bf16[384,1536]{1,0:T(8,128)(2,1)S(1)}, u32[]{:S(2)}, u32[]{:S(2)}) collective-permute-start(bf16[384,1536]{1,0:T(8,128)(2,1)} %up.5), channel_id=1, source_target_pairs={{0,16},{16,0},{1,17},{17,1},{2,18},{18,2},{3,19},{19,3},{4,20},{20... | collective-permute-start | bytes 3538952 | tf_op jit(solution)/shard_map/ppermute | solution.py:176
  9.4 32.6 %collective-permute-start.1 = (bf16[1536,384]{1,0:T(8,128)(2,1)}, bf16[1536,384]{1,0:T(8,128)(2,1)S(1)}, u32[]{:S(2)}, u32[]{:S(2)}) collective-permute-start(bf16[1536,384]{1,0:T(8,128)(2,1)} %down.5), channel_id=1, source_target_pairs={{0,16},{16,0},{1,17},{17,1},{2,18},{18,2},{3,19},{19,3},{4,20},{20... | collective-permute-start | bytes 3538952 | tf_op jit(solution)/shard_map/ppermute | solution.py:177
  14.2 27.7 %copy-start = (bf16[384,1536]{1,0:T(8,128)(2,1)S(1)}, bf16[384,1536]{1,0:T(8,128)(2,1)}, u32[]{:S(2)}) copy-start(bf16[384,1536]{1,0:T(8,128)(2,1)} %up.5) | copy-start | bytes 3538948
  14.2 27.8 %copy-start.1 = (bf16[1536,384]{1,0:T(8,128)(2,1)S(1)}, bf16[1536,384]{1,0:T(8,128)(2,1)}, u32[]{:S(2)}) copy-start(bf16[1536,384]{1,0:T(8,128)(2,1)} %down.5) | copy-start | bytes 3538948
  42.0 1.8 %copy-start.2 = (bf16[1536,384]{1,0:T(8,128)(2,1)}, bf16[1536,384]{1,0:T(8,128)(2,1)S(1)}, u32[]{:S(2)}) copy-start(bf16[1536,384]{1,0:T(8,128)(2,1)S(1)} %collective-permute-done.1.down2) | copy-start | bytes 3538948
  63.7 18.0 %copy-start.3 = (bf16[1536,384]{1,0:T(8,128)(2,1)S(1)}, bf16[1536,384]{1,0:T(8,128)(2,1)}, u32[]{:S(2)}) copy-start(bf16[1536,384]{1,0:T(8,128)(2,1)} %copy-done.2) | copy-start | bytes 3538948
  83.0 8.5 %collective-permute-start.2 = (bf16[128,1536]{1,0:T(8,128)(2,1)S(1)}, bf16[128,1536]{1,0:T(8,128)(2,1)S(1)}, u32[]{:S(2)}, u32[]{:S(2)}) collective-permute-start(bf16[128,1536]{1,0:T(8,128)(2,1)S(1)} %shard_map.79), channel_id=1, source_target_pairs={{0,1},{1,0},{2,3},{3,2},{4,5},{5,4},{6,7},{7,6},{8,9},{9,8},{10,11... | collective-permute-start | bytes 1179656 | tf_op jit(solution)/shard_map/ppermute | solution.py:207
  92.3 30.1 %all-to-all-start.2 = ((bf16[8,16,1536]{2,1,0:T(8,128)(2,1)}), bf16[8,16,1536]{2,1,0:T(8,128)(2,1)S(1)}, u32[]{:S(2)}, u32[]{:S(2)}) async-start(bf16[8,16,1536]{2,1,0:T(8,128)(2,1)} %bitcast.6), calls=%async_computation.2 | async-start | bytes 786432 | tf_op jit(solution)/shard_map/all_to_all | solution.py:210
  101.8 15.3 %collective-permute-start.3 = (bf16[256,1920]{1,0:T(8,128)(2,1)S(1)}, bf16[256,1920]{1,0:T(8,128)(2,1)S(1)}, u32[]{:S(2)}, u32[]{:S(2)}) collective-permute-start(bf16[256,1920]{1,0:T(8,128)(2,1)S(1)} %get-tuple-element.13), channel_id=1, source_target_pairs={{0,16},{16,0},{1,17},{17,1},{2,18},{18,2},{3,19},{19,3},{4,20},{20... | collective-permute-start | bytes 2949128 | tf_op jit(solution)/shard_map/ppermute | solution.py:217
  114.9 4.5 %collective-permute-start.4 = (bf16[256,1920]{1,0:T(8,128)(2,1)S(1)}, bf16[256,1920]{1,0:T(8,128)(2,1)S(1)}, u32[]{:S(2)}, u32[]{:S(2)}) collective-permute-start(bf16[256,1920]{1,0:T(8,128)(2,1)S(1)} %get-tuple-element.14), channel_id=1, source_target_pairs={{0,16},{16,0},{1,17},{17,1},{2,18},{18,2},{3,19},{19,3},{4,20},{20... | collective-permute-start | bytes 2949128 | tf_op jit(solution)/shard_map/ppermute | solution.py:217

commit v7 on v6

--- a/solution.py
+++ b/solution.py
@@ -13,9 +13,9 @@
 F32 = jnp.float32
 COEF = math.sqrt(2.0 / math.pi)
 CHIPS = [list(range(15, -1, -1))]
-TURN = 12
+TURN = 10
 RING = [(z + TURN) % 16 for z in range(16)]
-SHIFT = 4
+SHIFT = 5
 PARITIES = [[(TURN + p * (2 * SHIFT + 1) + 2 * q) % 16 for q in range(8)] for p in range(2)]
 SWAP = [(0, 1), (1, 0)]
 EVEN = [(z, z ^ 1) for z in range(16)]

time: 129 us -> 127 us (0.984)
  blocking collectives: 72.4 us -> 70.2 us
    all_gather x1, blocking collectives: 4.95 us -> 2.75 us  [per_device(): both = lax.all_gather(summed, 'core', axis=0, tiled=True)]
    all_to_all x1, starting transfers between devices: 8.27 us -> 9.92 us  [per_device(): lax.all_to_all(added, 'col', 0, 0, tiled=True, axis_index_groups=PARITIES)]
where the time goes in v7:
time: 127 us
  blocking collectives  70.2 us (55%)
  starting transfers between devices  37 us (29%)
  Pallas kernels  10.3 us (8%)
  waiting for transfers between devices  7.89 us (6%)
    all_gather x1, blocking collectives, per_device(): lax.all_gather(mine, 'col', axis=0, tiled=True, axis_index_groups=[RING])  27.7 us
    all_to_all x1, blocking collectives, per_device(): lax.all_to_all(partial, 'plane', 0, 0, tiled=True, axis_index_groups=CHIPS)  19.6 us
    all_to_all x1, blocking collectives, per_device(): lax.all_to_all(spread, 'plane', 0, 0, tiled=True, axis_index_groups=CHIPS)  18 us
    ppermute x2, starting transfers between devices, per_device(): others = [lax.ppermute(piece, 'core', SWAP) for piece in pieces]  14.5 us
    pallas_call x10, Pallas kernels, call(): pl.pallas_call(kernel, out_shape=out_shape, in_specs=specs, out_specs=[VM...  10.3 us
    all_to_all x1, starting transfers between devices, per_device(): lax.all_to_all(added, 'col', 0, 0, tiled=True, axis_index_groups=PARITIES)  9.92 us
    ppermute x1, starting transfers between devices, per_device(): up2 = lax.ppermute(up, 'core', SWAP)  8.79 us
    ppermute x1, waiting for transfers between devices, per_device(): came = lax.ppermute(send, 'col', EVEN)  5.35 us
  transfers between devices with their start and end apart: 6, of which 3 were waited for; matrix products, arithmetic and copies ran while one was open for 1% of the time, Pallas kernels for 4%

profile of v7, /device:TPU:1, one launch (start us, length us, event | category | flops | bytes accessed | tf_op | source)
XLA Modules:
  0.0 126.9 jit_solution(8926244418966300591)
XLA Ops:
  0.6 8.8 %collective-permute-start = (bf16[384,1536]{1,0:T(8,128)(2,1)}, bf16[384,1536]{1,0:T(8,128)(2,1)S(1)}, u32[]{:S(2)}, u32[]{:S(2)}) collective-permute-start(bf16[384,1536]{1,0:T(8,128)(2,1)} %up.5), channel_id=1, source_target_pairs={{0,16},{16,0},{1,17},{17,1},{2,18},{18,2},{3,19},{19,3},{4,20},{20... | collective-permute-start | bytes 3538952 | tf_op jit(solution)/shard_map/ppermute | solution.py:176
  9.4 1.9 %collective-permute-start.1 = (bf16[1536,384]{1,0:T(8,128)(2,1)}, bf16[1536,384]{1,0:T(8,128)(2,1)S(1)}, u32[]{:S(2)}, u32[]{:S(2)}) collective-permute-start(bf16[1536,384]{1,0:T(8,128)(2,1)} %down.5), channel_id=1, source_target_pairs={{0,16},{16,0},{1,17},{17,1},{2,18},{18,2},{3,19},{19,3},{4,20},{20... | collective-permute-start | bytes 3538952 | tf_op jit(solution)/shard_map/ppermute | solution.py:177
  11.4 0.8 pad_maximum_fusion
  12.1 2.1 %all_gather.9.pair = bf16[64,768]{1,0:T(8,128)(2,1)S(1)} all-gather(bf16[32,768]{1,0:T(8,128)(2,1)S(1)} %pad_maximum_fusion), channel_id=1, replica_groups=mesh['plane'=16,'core'=2,'col'=16] {'core'}, dimensions={0}, use_global_device_ids=true | all-gather | bytes 147456 | tf_op jit(solution)/shard_map/all_gather | solution.py:178
  14.2 0.0 copy-start
  14.2 0.0 copy-start.1
  14.3 27.7 %all_gather.10.panel = bf16[256,1536]{1,0:T(8,128)(2,1)S(1)} all-gather(bf16[16,1536]{1,0:T(8,128)(2,1)S(1)} %shard_map.75), channel_id=1, replica_groups={{10,11,12,13,14,15,0,1,2,3,4,5,6,7,8,9},{26,27,28,29,30,31,16,17,18,19,..., dimensions={0}, use_global_device_ids=true | all-gather | bytes 835584 | tf_op jit(solution)/shard_map/all_gather | solution.py:182
  42.0 0.0 collective-permute-done.up2
  42.0 0.0 collective-permute-done.1.down2
  42.0 0.0 copy-done
  42.0 0.0 copy-done.1
  42.0 0.0 copy-start.2
  42.0 1.8 %shard_map.76 = bf16[256,3072]{1,0:T(8,128)(2,1)S(1)} custom-call(bf16[256,1536]{1,0:T(8,128)(2,1)S(1)} %all_gather.10.panel, bf16[384,1536]{1,0:T(8,128)(2,1)S(1)} %copy-done, bf16[1536,384]{1,0:T(8,128)(2,1)S(1)} %copy-done.1, bf16[384,1536]{1,0:T(8,128)(2,1)S(1)} %collective-permute-done.up2, bf16[1536,384]{1,0:T(8,128)(2,1)S(1)} %collective-permute-done.1.down2), custom_call_target="tpu_custom_call" | custom-call | flops 1207959552 | bytes 7077888 | tf_op jit(solution)/shard_map/pallas_call | solution.py:44
  43.8 0.0 copy-done.2
  43.8 19.6 %all_to_all.34 = bf16[16,16,3072]{2,1,0:T(8,128)(2,1)S(1)} all-to-all(bf16[16,16,3072]{2,1,0:T(8,128)(2,1)S(1)} %bitcast.12), channel_id=1, replica_groups={{480,448,416,384,352,320,288,256,224,192,160,128,96,64,32,0},{481,449,4..., dimensions={0} | all-to-all | bytes 3145728 | tf_op jit(solution)/shard_map/all_to_all | solution.py:188
  63.4 0.3 shard_map.77
  63.7 0.0 copy-start.3
  63.8 18.0 %all_to_all.35 = bf16[16,16,3072]{2,1,0:T(8,128)(2,1)S(1)} all-to-all(bf16[16,16,3072]{2,1,0:T(8,128)(2,1)S(1)} %bitcast.14), channel_id=1, replica_groups={{480,448,416,384,352,320,288,256,224,192,160,128,96,64,32,0},{481,449,4..., dimensions={0} | all-to-all | bytes 3145728 | tf_op jit(solution)/shard_map/all_to_all | solution.py:190
  81.7 0.0 copy-done.3
  81.7 1.2 shard_map.79
  83.0 1.9 %collective-permute-start.2 = (bf16[128,1536]{1,0:T(8,128)(2,1)S(1)}, bf16[128,1536]{1,0:T(8,128)(2,1)S(1)}, u32[]{:S(2)}, u32[]{:S(2)}) collective-permute-start(bf16[128,1536]{1,0:T(8,128)(2,1)S(1)} %shard_map.79), channel_id=1, source_target_pairs={{0,1},{1,0},{2,3},{3,2},{4,5},{5,4},{6,7},{7,6},{8,9},{9,8},{10,11... | collective-permute-start | bytes 1179656 | tf_op jit(solution)/shard_map/ppermute | solution.py:207
  84.9 1.2 shard_map.78.keep
  86.1 5.4 %collective-permute-done.2.came = bf16[128,1536]{1,0:T(8,128)(2,1)S(1)} collective-permute-done((bf16[128,1536]{1,0:T(8,128)(2,1)S(1)}, bf16[128,1536]{1,0:T(8,128)(2,1)S(1)}, u32[]{:S(2)}, u32[]{:S(2)}) %collective-permute-start.2) | collective-permute-done | bytes 393248 | tf_op jit(solution)/shard_map/ppermute | solution.py:207
  91.5 0.8 shard_map.80._
  92.3 9.9 %all-to-all-start.2 = ((bf16[8,16,1536]{2,1,0:T(8,128)(2,1)}), bf16[8,16,1536]{2,1,0:T(8,128)(2,1)S(1)}, u32[]{:S(2)}, u32[]{:S(2)}) async-start(bf16[8,16,1536]{2,1,0:T(8,128)(2,1)} %bitcast.6), calls=%async_computation.2 | async-start | bytes 786432 | tf_op jit(solution)/shard_map/all_to_all | solution.py:210
  102.3 1.2 shard_map.81
  103.4 12.5 %collective-permute-start.3 = (bf16[256,1920]{1,0:T(8,128)(2,1)S(1)}, bf16[256,1920]{1,0:T(8,128)(2,1)S(1)}, u32[]{:S(2)}, u32[]{:S(2)}) collective-permute-start(bf16[256,1920]{1,0:T(8,128)(2,1)S(1)} %get-tuple-element.13), channel_id=1, source_target_pairs={{0,16},{16,0},{1,17},{17,1},{2,18},{18,2},{3,19},{19,3},{4,20},{20... | collective-permute-start | bytes 2949128 | tf_op jit(solution)/shard_map/ppermute | solution.py:217
  116.0 1.9 %collective-permute-start.4 = (bf16[256,1920]{1,0:T(8,128)(2,1)S(1)}, bf16[256,1920]{1,0:T(8,128)(2,1)S(1)}, u32[]{:S(2)}, u32[]{:S(2)}) collective-permute-start(bf16[256,1920]{1,0:T(8,128)(2,1)S(1)} %get-tuple-element.14), channel_id=1, source_target_pairs={{0,16},{16,0},{1,17},{17,1},{2,18},{18,2},{3,19},{19,3},{4,20},{20... | collective-permute-start | bytes 2949128 | tf_op jit(solution)/shard_map/ppermute | solution.py:217
  117.9 0.2 collective-permute-done.3.first
  118.1 2.3 %collective-permute-done.4.second = bf16[256,1920]{1,0:T(8,128)(2,1)S(1)} collective-permute-done((bf16[256,1920]{1,0:T(8,128)(2,1)S(1)}, bf16[256,1920]{1,0:T(8,128)(2,1)S(1)}, u32[]{:S(2)}, u32[]{:S(2)}) %collective-permute-start.4) | collective-permute-done | bytes 983072 | tf_op jit(solution)/shard_map/ppermute | solution.py:217
  120.4 3.0 %shard_map.82 = (bf16[384,1536]{1,0:T(8,128)(2,1)}, bf16[1536,384]{1,0:T(8,128)(2,1)}) custom-call(bf16[256,1536]{1,0:T(8,128)(2,1)S(1)} %all_gather.10.panel, bf16[256,3072]{1,0:T(8,128)(2,1)S(1)} %bitcast.11, bf16[256,1920]{1,0:T(8,128)(2,1)S(1)} %collective-permute-done.3.first, bf16[256,1920]{1,0:T(8,128)(2,1)S(1)} %collective-permute-done.4.second), custom_call_target="tpu_custom_call" | custom-call | flops 1207959552 | bytes 6684672 | tf_op jit(solution)/shard_map/pallas_call | solution.py:44
  123.4 0.0 all-to-all-done.2
  123.5 0.1 shard_map.83
  123.5 2.8 %all_gather.11.both = bf16[32,1536]{1,0:T(8,128)(2,1)S(1)} all-gather(bf16[16,1536]{1,0:T(8,128)(2,1)S(1)} %shard_map.83), channel_id=1, replica_groups=mesh['plane'=16,'core'=2,'col'=16] {'core'}, dimensions={0}, use_global_device_ids=true | all-gather | bytes 147456 | tf_op jit(solution)/shard_map/all_gather | solution.py:224
  126.3 0.6 shard_map.84
  (1 shorter events, 0.0 us)
Async XLA Ops:
  0.6 41.4 %collective-permute-start = (bf16[384,1536]{1,0:T(8,128)(2,1)}, bf16[384,1536]{1,0:T(8,128)(2,1)S(1)}, u32[]{:S(2)}, u32[]{:S(2)}) collective-permute-start(bf16[384,1536]{1,0:T(8,128)(2,1)} %up.5), channel_id=1, source_target_pairs={{0,16},{16,0},{1,17},{17,1},{2,18},{18,2},{3,19},{19,3},{4,20},{20... | collective-permute-start | bytes 3538952 | tf_op jit(solution)/shard_map/ppermute | solution.py:176
  9.4 32.6 %collective-permute-start.1 = (bf16[1536,384]{1,0:T(8,128)(2,1)}, bf16[1536,384]{1,0:T(8,128)(2,1)S(1)}, u32[]{:S(2)}, u32[]{:S(2)}) collective-permute-start(bf16[1536,384]{1,0:T(8,128)(2,1)} %down.5), channel_id=1, source_target_pairs={{0,16},{16,0},{1,17},{17,1},{2,18},{18,2},{3,19},{19,3},{4,20},{20... | collective-permute-start | bytes 3538952 | tf_op jit(solution)/shard_map/ppermute | solution.py:177
  14.2 27.7 %copy-start = (bf16[384,1536]{1,0:T(8,128)(2,1)S(1)}, bf16[384,1536]{1,0:T(8,128)(2,1)}, u32[]{:S(2)}) copy-start(bf16[384,1536]{1,0:T(8,128)(2,1)} %up.5) | copy-start | bytes 3538948
  14.2 27.8 %copy-start.1 = (bf16[1536,384]{1,0:T(8,128)(2,1)S(1)}, bf16[1536,384]{1,0:T(8,128)(2,1)}, u32[]{:S(2)}) copy-start(bf16[1536,384]{1,0:T(8,128)(2,1)} %down.5) | copy-start | bytes 3538948
  42.0 1.8 %copy-start.2 = (bf16[1536,384]{1,0:T(8,128)(2,1)}, bf16[1536,384]{1,0:T(8,128)(2,1)S(1)}, u32[]{:S(2)}) copy-start(bf16[1536,384]{1,0:T(8,128)(2,1)S(1)} %collective-permute-done.1.down2) | copy-start | bytes 3538948
  63.7 18.0 %copy-start.3 = (bf16[1536,384]{1,0:T(8,128)(2,1)S(1)}, bf16[1536,384]{1,0:T(8,128)(2,1)}, u32[]{:S(2)}) copy-start(bf16[1536,384]{1,0:T(8,128)(2,1)} %copy-done.2) | copy-start | bytes 3538948
  83.0 8.5 %collective-permute-start.2 = (bf16[128,1536]{1,0:T(8,128)(2,1)S(1)}, bf16[128,1536]{1,0:T(8,128)(2,1)S(1)}, u32[]{:S(2)}, u32[]{:S(2)}) collective-permute-start(bf16[128,1536]{1,0:T(8,128)(2,1)S(1)} %shard_map.79), channel_id=1, source_target_pairs={{0,1},{1,0},{2,3},{3,2},{4,5},{5,4},{6,7},{7,6},{8,9},{9,8},{10,11... | collective-permute-start | bytes 1179656 | tf_op jit(solution)/shard_map/ppermute | solution.py:207
  92.3 31.1 %all-to-all-start.2 = ((bf16[8,16,1536]{2,1,0:T(8,128)(2,1)}), bf16[8,16,1536]{2,1,0:T(8,128)(2,1)S(1)}, u32[]{:S(2)}, u32[]{:S(2)}) async-start(bf16[8,16,1536]{2,1,0:T(8,128)(2,1)} %bitcast.6), calls=%async_computation.2 | async-start | bytes 786432 | tf_op jit(solution)/shard_map/all_to_all | solution.py:210
  103.4 14.7 %collective-permute-start.3 = (bf16[256,1920]{1,0:T(8,128)(2,1)S(1)}, bf16[256,1920]{1,0:T(8,128)(2,1)S(1)}, u32[]{:S(2)}, u32[]{:S(2)}) collective-permute-start(bf16[256,1920]{1,0:T(8,128)(2,1)S(1)} %get-tuple-element.13), channel_id=1, source_target_pairs={{0,16},{16,0},{1,17},{17,1},{2,18},{18,2},{3,19},{19,3},{4,20},{20... | collective-permute-start | bytes 2949128 | tf_op jit(solution)/shard_map/ppermute | solution.py:217
  116.0 4.5 %collective-permute-start.4 = (bf16[256,1920]{1,0:T(8,128)(2,1)S(1)}, bf16[256,1920]{1,0:T(8,128)(2,1)S(1)}, u32[]{:S(2)}, u32[]{:S(2)}) collective-permute-start(bf16[256,1920]{1,0:T(8,128)(2,1)S(1)} %get-tuple-element.14), channel_id=1, source_target_pairs={{0,16},{16,0},{1,17},{17,1},{2,18},{18,2},{3,19},{19,3},{4,20},{20... | collective-permute-start | bytes 2949128 | tf_op jit(solution)/shard_map/ppermute | solution.py:217
